TPU v7x, 128 devices: a whole 4x4x4 slice. The times are simulated.
128 devices in a mesh: batch: 2 (over y_lo), seq: 16 (over y_hi, x, core), tensor: 4 (over z).
Axes of the slice: x: 4, y: 4 (y_hi: 2, y_lo: 2; y = y_hi * 2 + y_lo), z: 4, core: 2. Of those that a mesh axis runs over, the one named last changes fastest.
Arguments:
- hidden_in: float32 [2, 2, 2048, 1024], P(None, 'batch', 'seq'), may hold values from -6 to 6
- document_ids: int32 [2, 2, 2048], P(None, 'batch', 'seq'), may hold values from 0 to 2, as said below
- first_gain: float32 [2, 1024], replicated, may hold values from 0.1 to 1.9
- first_shift: float32 [2, 1024], replicated, may hold values from -1.75 to 1.75
- second_gain: float32 [2, 1024], replicated, may hold values from 0.1 to 1.9
- second_shift: float32 [2, 1024], replicated, may hold values from -1.75 to 1.75
- attn_weight: bfloat16 [2, 1024, 3072], P(None, ('batch', 'seq'), 'tensor'), may hold values from -0.1875 to 0.1875
- attn_bias: float32 [2, 3072], P(None, 'tensor'), may hold values from -1.75 to 1.75
- dense_weight: bfloat16 [2, 1024, 1024], P(None, 'tensor', ('batch', 'seq')), may hold values from -1.5 to 1.5
- dense_bias: float32 [2, 1024], replicated, may hold values from -1.75 to 1.75
- expand_weight: bfloat16 [2, 1024, 4096], P(None, ('batch', 'seq'), 'tensor'), may hold values from -0.1875 to 0.1875
- expand_bias: float32 [2, 4096], P(None, 'tensor'), may hold values from -3 to 3
- shrink_weight: bfloat16 [2, 4096, 1024], P(None, 'tensor', ('batch', 'seq')), may hold values from -0.125 to 0.125
- shrink_bias: float32 [2, 1024], replicated, may hold values from -1.75 to 1.75
- output_grad: float32 [2, 2, 2048, 1024], P(None, 'batch', 'seq'), may hold values from -6 to 6
Outputs:
- hidden_out: float32 [2, 2, 2048, 1024], P(None, 'batch', 'seq')
- input_grad: float32 [2, 2, 2048, 1024], P(None, 'batch', 'seq')
- grad_first_gain: float32 [2, 1024], replicated
- grad_first_shift: float32 [2, 1024], replicated
- grad_second_gain: float32 [2, 1024], replicated
- grad_second_shift: float32 [2, 1024], replicated
- grad_attn_weight: float32 [2, 1024, 3072], P(None, ('batch', 'seq'), 'tensor')
- grad_attn_bias: float32 [2, 3072], P(None, 'tensor')
- grad_dense_weight: float32 [2, 1024, 1024], P(None, 'tensor', ('batch', 'seq'))
- grad_dense_bias: float32 [2, 1024], replicated
- grad_expand_weight: float32 [2, 1024, 4096], P(None, ('batch', 'seq'), 'tensor')
- grad_expand_bias: float32 [2, 4096], P(None, 'tensor')
- grad_shrink_weight: float32 [2, 4096, 1024], P(None, 'tensor', ('batch', 'seq'))
- grad_shrink_bias: float32 [2, 1024], replicated
Inputs may be any that keep to these rules, and one draw needn't show every extreme that they name: `document_ids`: in every sequence the ids never fall and take each of the values 0, 1 and 2 on at least one token; id 1 begins within the first 128 tokens and ends within the last 128 tokens.
All inputs are finite; a program needn't handle non-finite values.
Results may differ from a plain program's by a relative error of at most 0.025.
Values may be sent and summed in bfloat16 or wider, within the bound.
A program may use at most 192 MiB of HBM per device.

v0:
```python
import jax
import jax.numpy as jnp
from jax import lax
from jax.sharding import PartitionSpec as P

HEAD = 64
ROT = 16
LAYERS = 2


MASKED = -1000000000.0


def laid_out(parts, dim):
    parts = jnp.moveaxis(parts, 0, dim)
    dims = parts.shape
    return parts.reshape(*dims[:dim], dims[dim] * dims[dim + 1], *dims[dim + 2 :])


def copy_for_each(value, axis):
    copies = jnp.broadcast_to(value, (lax.axis_size(axis), *value.shape))
    return lax.all_to_all(copies, axis, split_axis=0, concat_axis=0, tiled=True)


def collect(value, axis, dim):
    return laid_out(copy_for_each(value, axis), dim)


def gather_turned(arrays, axis, dims):
    turned = [jnp.moveaxis(a, dim, 0) for a, dim in zip(arrays, dims)]
    both = jnp.concatenate([t.reshape(len(t), -1) for t in turned], axis=1)
    filled, at, finished = (lax.all_gather(both, axis, axis=0, tiled=True), 0, [])
    for t, dim in zip(turned, dims):
        section = filled[:, at : at + t[0].size].reshape(-1, *t.shape[1:])
        finished.append(jnp.moveaxis(section, 0, dim))
        at += t[0].size
    return tuple(finished)


def in_one_piece(arrays, axis, dim, along):
    ends, at = ([], 0)
    for a in arrays[:-1]:
        at += a.shape[along]
        ends.append(at)
    both = jnp.concatenate(arrays, axis=along)
    return tuple(jnp.split(lax.all_gather(both, axis, axis=dim, tiled=True), ends, axis=along))


def over_copies(value, axis):
    return copy_for_each(value, axis).astype(jnp.float32).sum(axis=0)


def split_up(value, dim, length):
    before, after = (value.shape[:dim], value.shape[dim + 1 :])
    return jnp.moveaxis(value.reshape(*before, length, -1, *after), dim, 0)


def sum_packed(arrays, axis, dims):
    length = lax.axis_size(axis)
    parts = [split_up(a, dim, length) for a, dim in zip(arrays, dims)]
    lines = jnp.concatenate([b.reshape(length, -1) for b in parts], axis=1)
    span = max(16, -(-lines.shape[1] // 1024) * 8)
    lines = jnp.pad(lines, ((0, 0), (0, span * 128 - lines.shape[1]))).reshape(-1, 128)
    vector, at, finished = (lax.psum_scatter(lines, axis, tiled=True).reshape(-1), 0, [])
    for b in parts:
        part = b[0]
        finished.append(vector[at : at + part.size].reshape(part.shape))
        at += part.size
    return tuple(finished)


def layer_norm(values, gain, shift):
    centre = jnp.mean(values, axis=-1, keepdims=True)
    centred = values - centre
    spread = jnp.mean(centred * centred, axis=-1, keepdims=True)
    return centred * lax.rsqrt(spread + 1e-05) * gain + shift


def rotary_angles(positions):
    inverse = 10000.0 ** (-jnp.arange(0, ROT, 2).astype(jnp.float32) / ROT)
    return positions.astype(jnp.float32)[:, None] * inverse[None, :]


def rotate(vectors, angles):
    halfway = ROT // 2
    cosine = jnp.cos(angles)
    sine_part = jnp.sin(angles)
    cosine = jnp.concatenate([cosine, cosine], axis=-1)[:, None, :]
    sine_part = jnp.concatenate([sine_part, sine_part], axis=-1)[:, None, :]
    leading = vectors[..., :ROT]
    turned = jnp.concatenate([-leading[..., halfway:], leading[..., :halfway]], axis=-1)
    return jnp.concatenate([leading * cosine + turned * sine_part, vectors[..., ROT:]], axis=-1)


def masked_scores(query_blocks, key_blocks, allowed, scaling):
    raw_scores = (
        jnp.einsum("sqhd,skhd->shqk", query_blocks, key_blocks, preferred_element_type=jnp.float32)
        * scaling
    )
    return jnp.where(allowed[:, None], raw_scores, MASKED)


def add_up(running, fresh):
    if running is None:
        return fresh
    return jax.tree.map(lambda left, right: left + right, running, fresh)


def stack_layers(per_layer):
    return tuple(
        (
            jnp.stack([entry[which_one] for entry in per_layer])
            for which_one in range(len(per_layer[0]))
        )
    )


def local(
    hidden_in,
    document_ids,
    first_gain,
    first_shift,
    second_gain,
    second_shift,
    attn_weight,
    attn_bias,
    dense_weight,
    dense_bias,
    expand_weight,
    expand_bias,
    shrink_weight,
    shrink_bias,
    output_grad,
):
    micro_count, seq_count, piece_len, model_width = hidden_in.shape
    row_count = seq_count * piece_len
    local_width = attn_weight.shape[2] // 3
    local_heads = local_width // HEAD
    scaling = HEAD ** (-0.5)
    total_len = piece_len * lax.axis_size("seq")
    piece_start = lax.axis_index("seq") * piece_len
    query_place = piece_start + jnp.arange(piece_len, dtype=jnp.int32)
    key_place = jnp.arange(total_len, dtype=jnp.int32)
    angles = rotary_angles(jnp.tile(query_place, seq_count))
    causal = query_place[:, None] >= key_place[None, :]
    causal_back = key_place[:, None] >= query_place[None, :]
    key_idents = collect(document_ids, "seq", 2)
    kept_weights = [
        gather_turned(
            (
                attn_weight[layer_at],
                dense_weight[layer_at],
                expand_weight[layer_at],
                shrink_weight[layer_at],
            ),
            ("batch", "seq"),
            (0, 1, 0, 1),
        )
        for layer_at in range(LAYERS)
    ]

    def backward_layer(grad_out, kept, gathered, allowed, allowed_back, layer_at):
        (
            hidden,
            normed_one,
            normed_two,
            query_blocks,
            far_key_heads,
            far_value_heads,
            log_totals,
            context,
            expanded,
            active,
        ) = kept
        joint_matrix, dense_matrix, expand_matrix, shrink_matrix = gathered
        grad_branch = grad_out.astype(jnp.bfloat16)
        branch_total = jnp.sum(grad_branch.astype(jnp.float32), axis=0)
        grad_dense_matrix = jnp.einsum(
            "rc,rd->cd", context, grad_branch, preferred_element_type=jnp.float32
        )
        grad_shrink_matrix = jnp.einsum(
            "rf,rd->fd", active, grad_branch, preferred_element_type=jnp.float32
        )
        grad_context = jnp.einsum(
            "rd,cd->rc", grad_branch, dense_matrix, preferred_element_type=jnp.float32
        ).astype(jnp.bfloat16)
        grad_active = jnp.einsum(
            "rd,fd->rf", grad_branch, shrink_matrix, preferred_element_type=jnp.float32
        )
        gelu_back = jax.vjp(lambda inner: jax.nn.gelu(inner, approximate=False), expanded)[1]
        grad_expanded = gelu_back(grad_active)[0].astype(jnp.bfloat16)
        grad_expand_vector = jnp.sum(grad_expanded.astype(jnp.float32), axis=0)
        grad_expand_matrix = jnp.einsum(
            "rd,rf->df", normed_two, grad_expanded, preferred_element_type=jnp.float32
        )
        part_two = jnp.einsum(
            "rf,df->rd", grad_expanded, expand_matrix, preferred_element_type=jnp.float32
        )
        scores = masked_scores(query_blocks, far_key_heads, allowed, scaling)
        softmaxed = jnp.exp(scores - log_totals)
        grad_ctx_heads = grad_context.reshape(seq_count, piece_len, local_heads, HEAD)
        grad_softmaxed = jnp.einsum(
            "sqhd,skhd->shqk", grad_ctx_heads, far_value_heads, preferred_element_type=jnp.float32
        )
        row_terms = jnp.sum(softmaxed * grad_softmaxed, axis=-1, keepdims=True)
        grad_scores = (softmaxed * (grad_softmaxed - row_terms)).astype(jnp.bfloat16)
        grad_queries = (
            jnp.einsum(
                "shqk,skhd->sqhd", grad_scores, far_key_heads, preferred_element_type=jnp.float32
            )
            * scaling
        )
        all_queries, all_grad_ctx = in_one_piece((query_blocks, grad_ctx_heads), "seq", 1, 0)
        all_log_totals, all_row_terms = in_one_piece((log_totals, row_terms), "seq", 2, 0)
        mine_keys = lax.dynamic_slice_in_dim(far_key_heads, piece_start, piece_len, 1)
        mine_values = lax.dynamic_slice_in_dim(far_value_heads, piece_start, piece_len, 1)
        back_scores = masked_scores(all_queries, mine_keys, allowed_back, scaling)
        back_soft = jnp.exp(back_scores - all_log_totals)
        back_grad_soft = jnp.einsum(
            "sqhd,skhd->shqk", all_grad_ctx, mine_values, preferred_element_type=jnp.float32
        )
        back_grad_scores = (back_soft * (back_grad_soft - all_row_terms)).astype(jnp.bfloat16)
        own_key_heads = (
            jnp.einsum(
                "shqk,sqhd->skhd", back_grad_scores, all_queries, preferred_element_type=jnp.float32
            )
            * scaling
        )
        own_value_heads = jnp.einsum(
            "shqk,sqhd->skhd",
            back_soft.astype(jnp.bfloat16),
            all_grad_ctx,
            preferred_element_type=jnp.float32,
        )
        own_keys = own_key_heads.reshape(seq_count, piece_len, local_width)
        own_values = own_value_heads.reshape(seq_count, piece_len, local_width)
        grad_query_raw = rotate(grad_queries.reshape(row_count, local_heads, HEAD), -angles)
        grad_key_raw = rotate(own_keys.reshape(row_count, local_heads, HEAD), -angles)
        grad_value_raw = own_values.reshape(row_count, local_heads, HEAD)
        grad_joint = (
            jnp.stack([grad_query_raw, grad_key_raw, grad_value_raw], axis=2)
            .reshape(row_count, 3 * local_width)
            .astype(jnp.bfloat16)
        )
        grad_joint_vector = jnp.sum(grad_joint.astype(jnp.float32), axis=0)
        grad_joint_matrix = jnp.einsum(
            "rd,rc->dc", normed_one, grad_joint, preferred_element_type=jnp.float32
        )
        part_one = jnp.einsum(
            "rc,dc->rd", grad_joint, joint_matrix, preferred_element_type=jnp.float32
        )
        grad_one, grad_two = (
            over_copies(part_one.astype(jnp.bfloat16), "tensor").astype(jnp.float32),
            over_copies(part_two.astype(jnp.bfloat16), "tensor").astype(jnp.float32),
        )
        norm_back_one = jax.vjp(layer_norm, hidden, first_gain[layer_at], first_shift[layer_at])[1]
        norm_back_two = jax.vjp(layer_norm, hidden, second_gain[layer_at], second_shift[layer_at])[
            1
        ]
        input_one, gain_one, shift_one = norm_back_one(grad_one)
        input_two, gain_two, shift_two = norm_back_two(grad_two)
        grad_in = grad_out + input_one + input_two
        big_terms = (grad_joint_matrix, grad_dense_matrix, grad_expand_matrix, grad_shrink_matrix)
        small_terms = (
            gain_one,
            shift_one,
            gain_two,
            shift_two,
            grad_joint_vector,
            branch_total,
            grad_expand_vector,
            branch_total,
        )
        return (grad_in, big_terms, small_terms)

    outputs = []
    input_grads = []
    big_sums = [None] * LAYERS
    small_sums = [None] * LAYERS
    for micro_at in range(micro_count):
        hidden = hidden_in[micro_at].reshape(row_count, model_width)
        own_idents = document_ids[micro_at]
        allowed = causal[None] & (own_idents[:, :, None] == key_idents[micro_at][:, None, :])
        allowed_back = causal_back[None] & (
            key_idents[micro_at][:, :, None] == own_idents[:, None, :]
        )
        kept_layers = []
        for layer_at in range(LAYERS):
            gathered = kept_weights[layer_at]
            (
                forward_joint_matrix,
                forward_dense_matrix,
                forward_expand_matrix,
                forward_shrink_matrix,
            ) = gathered
            forward_normed_one = layer_norm(
                hidden, first_gain[layer_at], first_shift[layer_at]
            ).astype(jnp.bfloat16)
            forward_normed_two = layer_norm(
                hidden, second_gain[layer_at], second_shift[layer_at]
            ).astype(jnp.bfloat16)
            projected = (
                jnp.dot(
                    forward_normed_one, forward_joint_matrix, preferred_element_type=jnp.float32
                )
                + attn_bias[layer_at]
            )
            projected = projected.reshape(row_count, local_heads, 3, HEAD)
            queries = rotate(projected[:, :, 0], angles).astype(jnp.bfloat16)
            key_heads = rotate(projected[:, :, 1], angles).astype(jnp.bfloat16)
            value_heads = projected[:, :, 2].astype(jnp.bfloat16)
            far_keys, far_values = in_one_piece(
                (
                    key_heads.reshape(seq_count, piece_len, local_width),
                    value_heads.reshape(seq_count, piece_len, local_width),
                ),
                "seq",
                1,
                0,
            )
            forward_query_blocks = queries.reshape(seq_count, piece_len, local_heads, HEAD)
            forward_far_key_heads = far_keys.reshape(seq_count, total_len, local_heads, HEAD)
            forward_far_value_heads = far_values.reshape(seq_count, total_len, local_heads, HEAD)
            forward_scores = masked_scores(
                forward_query_blocks, forward_far_key_heads, allowed, scaling
            )
            highest = jnp.max(forward_scores, axis=-1, keepdims=True)
            exponent = jnp.exp(forward_scores - highest)
            totals = jnp.sum(exponent, axis=-1, keepdims=True)
            forward_softmaxed = exponent / totals
            forward_log_totals = highest + jnp.log(totals)
            forward_context = jnp.einsum(
                "shqk,skhd->sqhd",
                forward_softmaxed.astype(jnp.bfloat16),
                forward_far_value_heads,
                preferred_element_type=jnp.float32,
            )
            forward_context = forward_context.reshape(row_count, local_width).astype(jnp.bfloat16)
            forward_expanded = (
                jnp.dot(
                    forward_normed_two, forward_expand_matrix, preferred_element_type=jnp.float32
                )
                + expand_bias[layer_at]
            )
            forward_active = jax.nn.gelu(forward_expanded, approximate=False).astype(jnp.bfloat16)
            partial_sum = jnp.dot(
                forward_context, forward_dense_matrix, preferred_element_type=jnp.float32
            ) + jnp.dot(forward_active, forward_shrink_matrix, preferred_element_type=jnp.float32)
            branch = (
                over_copies(partial_sum.astype(jnp.bfloat16), "tensor").astype(jnp.float32)
                + dense_bias[layer_at]
                + shrink_bias[layer_at]
            )
            forward_kept = (
                hidden,
                forward_normed_one,
                forward_normed_two,
                forward_query_blocks,
                forward_far_key_heads,
                forward_far_value_heads,
                forward_log_totals,
                forward_context,
                forward_expanded,
                forward_active,
            )
            hidden, kept = (hidden + branch, forward_kept)
            kept_layers.append(kept)
        outputs.append(hidden.reshape(seq_count, piece_len, model_width))
        grad_flow = output_grad[micro_at].reshape(row_count, model_width)
        micro_big = [None] * LAYERS
        for layer_at in reversed(range(LAYERS)):
            gathered = kept_weights[layer_at]
            grad_flow, big_terms, small_terms = backward_layer(
                grad_flow, kept_layers[layer_at], gathered, allowed, allowed_back, layer_at
            )
            micro_big[layer_at] = big_terms
            small_sums[layer_at] = add_up(small_sums[layer_at], small_terms)
        input_grads.append(grad_flow.reshape(seq_count, piece_len, model_width))
        big_sums = [add_up(big_sums[layer_at], micro_big[layer_at]) for layer_at in range(LAYERS)]
    stacked_big = stack_layers(big_sums)
    weight_grads = tuple(
        (
            part.astype(jnp.float32)
            for part in sum_packed(
                (
                    stacked_big[0].astype(jnp.bfloat16),
                    stacked_big[1].astype(jnp.bfloat16),
                    stacked_big[2].astype(jnp.bfloat16),
                    stacked_big[3].astype(jnp.bfloat16),
                ),
                ("batch", "seq"),
                (1, 2, 1, 2),
            )
        )
    )
    stacked_small = stack_layers(small_sums)
    small = (
        over_copies(stacked_small[0].astype(jnp.bfloat16), ("batch", "seq")).astype(jnp.float32),
        over_copies(stacked_small[1].astype(jnp.bfloat16), ("batch", "seq")).astype(jnp.float32),
        over_copies(stacked_small[2].astype(jnp.bfloat16), ("batch", "seq")).astype(jnp.float32),
        over_copies(stacked_small[3].astype(jnp.bfloat16), ("batch", "seq")).astype(jnp.float32),
        over_copies(stacked_small[4].astype(jnp.bfloat16), ("batch", "seq")).astype(jnp.float32),
        over_copies(stacked_small[5].astype(jnp.bfloat16), ("batch", "seq")).astype(jnp.float32),
        over_copies(stacked_small[6].astype(jnp.bfloat16), ("batch", "seq")).astype(jnp.float32),
        over_copies(stacked_small[7].astype(jnp.bfloat16), ("batch", "seq")).astype(jnp.float32),
    )
    return (
        jnp.stack(outputs),
        jnp.stack(input_grads),
        small[0],
        small[1],
        small[2],
        small[3],
        weight_grads[0],
        small[4],
        weight_grads[1],
        small[5],
        weight_grads[2],
        small[6],
        weight_grads[3],
        small[7],
    )


def solution(mesh):
    placed = (
        P(None, "batch", "seq", None),
        P(None, "batch", "seq"),
        P(),
        P(),
        P(),
        P(),
        P(None, ("batch", "seq"), "tensor"),
        P(None, "tensor"),
        P(None, "tensor", ("batch", "seq")),
        P(),
        P(None, ("batch", "seq"), "tensor"),
        P(None, "tensor"),
        P(None, "tensor", ("batch", "seq")),
        P(),
        P(None, "batch", "seq", None),
    )
    return jax.shard_map(
        local,
        mesh=mesh,
        in_specs=placed,
        out_specs=(
            P(None, "batch", "seq", None),
            P(None, "batch", "seq", None),
            P(),
            P(),
            P(),
            P(),
            P(None, ("batch", "seq"), "tensor"),
            P(None, "tensor"),
            P(None, "tensor", ("batch", "seq")),
            P(),
            P(None, ("batch", "seq"), "tensor"),
            P(None, "tensor"),
            P(None, "tensor", ("batch", "seq")),
            P(),
        ),
        check_vma=False,
    )
```

profile of v0, /device:TPU:24, one launch (start us, length us, event | category | flops | bytes accessed | tf_op | source)
XLA Modules:
  0.0 1011.4 jit_solution(4298802977465602093)
XLA Ops:
  18.0 58.3 %all-gather.11.cloned.1.call-done = bf16[1024,3072]{1,0:T(8,128)(2,1)} async-done(((bf16[32,3072]{1,0:T(8,128)(2,1)}), bf16[1024,3072]{1,0:T(8,128)(2,1)}) %all-gather.11.cloned.1.call-update) | async-done | bytes 6291472 | tf_op jit(solution)/shard_map/all_gather | solution.py:32
  83.6 6.3 all-to-all-start
  101.2 28.6 %all-gather.19.cloned.1.call-done = bf16[2,2048,256]{1,2,0:T(8,128)(2,1)} async-done(((bf16[2,128,256]{1,2,0:T(8,128)(2,1)}), bf16[2,2048,256]{1,2,0:T(8,128)(2,1)}) %all-gather.19.cloned.1.call-update) | async-done | bytes 2097168 | tf_op jit(solution)/shard_map/all_gather | solution.py:46
  145.9 35.1 %all-gather.13.cloned.1.call-done = bf16[2,2048,256]{1,2,0:T(8,128)(2,1)} async-done(((bf16[2,128,256]{1,2,0:T(8,128)(2,1)}), bf16[2,2048,256]{1,2,0:T(8,128)(2,1)}) %all-gather.13.cloned.1.call-update) | async-done | bytes 2097168 | tf_op jit(solution)/shard_map/all_gather | solution.py:46
  198.9 14.3 %all-to-all-done.1 = bf16[4,128,1024]{2,1,0:T(8,128)(2,1)} async-done(((bf16[4,128,1024]{2,1,0:T(8,128)(2,1)}), bf16[4,128,1024]{2,1,0:T(8,128)(2,1)}, u32[]{:S(2)}, u32[]{:S(2)}) %all-to-all-start.1) | async-done | bytes 1048608 | tf_op jit(solution)/shard_map/all_to_all | solution.py:22
  216.5 29.7 %all-gather.15.cloned.1.call-done = bf16[1024,3072]{1,0:T(8,128)(2,1)} async-done(((bf16[32,3072]{1,0:T(8,128)(2,1)}), bf16[1024,3072]{1,0:T(8,128)(2,1)}) %all-gather.15.cloned.1.call-update) | async-done | bytes 6291472 | tf_op jit(solution)/shard_map/all_gather | solution.py:32
  349.8 22.4 %all_gather.53 = f32[2,4,2048,1]{2,1,3,0:T(4,128)S(1)} all-gather(f32[2,4,128,1]{2,1,3,0:T(4,128)S(1)} %pad_maximum_fusion.25), channel_id=1, replica_groups=mesh['batch'=2,'seq'=16,'tensor'=4] {'seq'}, dimensions={2}, use_global_device_ids=true | all-gather | bytes 69632 | tf_op jit(solution)/shard_map/all_gather | solution.py:46
  386.0 31.4 %all-gather.17.cloned.1.call-done = bf16[2,2048,256]{1,2,0:T(8,128)(2,1)} async-done(((bf16[2,128,256]{1,2,0:T(8,128)(2,1)}), bf16[2,2048,256]{1,2,0:T(8,128)(2,1)}) %all-gather.17.cloned.1.call-update) | async-done | bytes 2097168 | tf_op jit(solution)/shard_map/all_gather | solution.py:46
  424.0 23.0 %all_gather.49 = f32[2,4,2048,1]{2,1,3,0:T(4,128)S(1)} all-gather(f32[2,4,128,1]{2,1,3,0:T(4,128)S(1)} %pad_maximum_fusion.23), channel_id=1, replica_groups=mesh['batch'=2,'seq'=16,'tensor'=4] {'seq'}, dimensions={2}, use_global_device_ids=true | all-gather | bytes 69632 | tf_op jit(solution)/shard_map/all_gather | solution.py:46
  449.4 19.1 %all-gather.23.cloned.1.call-done = bf16[2,2048,4,64]{1,3,2,0:T(8,128)(2,1)} async-done(((bf16[2,128,4,64]{1,3,2,0:T(8,128)(2,1)}), bf16[2,2048,4,64]{1,3,2,0:T(8,128)(2,1)}) %all-gather.23.cloned.1.call-update) | async-done | bytes 2097168 | tf_op jit(solution)/shard_map/all_gather | solution.py:46
  503.4 7.4 all-to-all-done.9
  596.2 24.9 %all_gather.55 = f32[2,4,2048,1]{2,1,3,0:T(4,128)} all-gather(f32[2,4,128,1]{2,1,3,0:T(4,128)S(1)} %copy-done.176), channel_id=1, replica_groups=mesh['batch'=2,'seq'=16,'tensor'=4] {'seq'}, dimensions={2}, use_global_device_ids=true | all-gather | bytes 69632 | tf_op jit(solution)/shard_map/all_gather | solution.py:46
  626.7 14.4 %copy.204 = bf16[32,2,1024,32]{3,2,1,0:T(8,128)(2,1)} copy(bf16[32,2,1024,32]{2,3,0,1:T(8,128)(2,1)} %maximum_bitcast_fusion) | data formatting | bytes 8388608 | tf_op jit(solution)/shard_map/transpose | solution.py:55
  641.1 21.1 %reshape.2666 = bf16[32,65536]{1,0:T(8,128)(2,1)} reshape(bf16[32,2,1024,32]{3,2,1,0:T(8,128)(2,1)} %copy.204) | data formatting | bytes 8388608 | tf_op jit(solution)/shard_map/reshape | solution.py:61
  662.2 20.8 %all_gather.51 = f32[2,4,2048,1]{2,1,3,0:T(4,128)} all-gather(f32[2,4,128,1]{2,1,3,0:T(4,128)S(1)} %copy-done.175), channel_id=1, replica_groups=mesh['batch'=2,'seq'=16,'tensor'=4] {'seq'}, dimensions={2}, use_global_device_ids=true | all-gather | bytes 69632 | tf_op jit(solution)/shard_map/all_gather | solution.py:46
  699.8 10.4 %all-to-all-done.8 = bf16[4,128,1024]{2,1,0:T(8,128)(2,1)} async-done(((bf16[4,128,1024]{2,1,0:T(8,128)(2,1)}), bf16[4,128,1024]{2,1,0:T(8,128)(2,1)}, u32[]{:S(2)}, u32[]{:S(2)}) %all-to-all-start.8) | async-done | bytes 1048608 | tf_op jit(solution)/shard_map/all_to_all | solution.py:22
  753.2 5.9 all-to-all-done.11
  772.6 6.9 all-to-all-done.7
  801.8 5.9 reshape.2664
  807.7 19.8 %pad_maximum_fusion = bf16[32,196608]{1,0:T(8,128)(2,1)} fusion(bf16[32,65536]{1,0:T(8,128)(2,1)} %reshape.2666, bf16[32,65536]{1,0:T(8,128)(2,1)} %bitcast.603, bf16[32,16384]{1,0:T(8,128)(2,1)S(1)} %reshape.2664, bf16[32,49152]{1,0:T(8,128)(2,1)} %bitcast.604), kind=kLoop, calls=%fused_computation | loop fusion | flops 50331648 | bytes 25165824 | tf_op jit(solution)/shard_map/concatenate | solution.py:61
  827.5 12.1 %reshape.2667 = bf16[49152,128]{1,0:T(8,128)(2,1)} reshape(bf16[32,196608]{1,0:T(8,128)(2,1)} %pad_maximum_fusion) | data formatting | bytes 25165824 | tf_op jit(solution)/shard_map/reshape | solution.py:63
  854.6 8.1 all-to-all-done.4
  868.4 11.6 %all-to-all-done.2 = bf16[4,128,1024]{2,1,0:T(8,128)(2,1)} async-done(((bf16[4,128,1024]{2,1,0:T(8,128)(2,1)}), bf16[4,128,1024]{2,1,0:T(8,128)(2,1)}, u32[]{:S(2)}, u32[]{:S(2)}) %all-to-all-start.2) | async-done | bytes 1048608 | tf_op jit(solution)/shard_map/all_to_all | solution.py:22
  880.7 6.3 all-to-all-start.18
  887.2 6.3 all-to-all-done.18
  894.2 5.6 all-to-all-start.19
  907.1 6.5 all-to-all-start.16
  913.8 6.5 all-to-all-done.16
  921.0 5.7 all-to-all-start.17
  933.7 5.9 all-to-all-start.15
  953.3 5.6 all-to-all-done.14
  972.0 25.4 %reduce-scatter.2.cloned.1.call-done = bf16[1536,128]{1,0:T(8,128)(2,1)} async-done(((bf16[49152,128]{1,0:T(8,128)(2,1)}), bf16[1536,128]{1,0:T(8,128)(2,1)}) %reduce-scatter.2.cloned.1.call-update) | async-done | bytes 393232 | tf_op jit(solution)/shard_map/reduce_scatter | solution.py:64
  (862 shorter events, 482.1 us)
Async XLA Ops:
  7.2 69.1 %all-gather.11.cloned.1.call-start = ((), (), s32[]{:S(2)}) async-start(), calls=%async_computation.21 | async-start | bytes 6488064 | tf_op jit(solution)/shard_map/all_gather | solution.py:32
  11.4 118.4 %all-gather.19.cloned.1.call-start = ((), (), s32[]{:S(2)}) async-start(), calls=%async_computation.25 | async-start | bytes 2228224 | tf_op jit(solution)/shard_map/all_gather | solution.py:46
  13.0 233.2 %copy-start.205 = (f32[768]{0:T(1024)}, f32[768]{0:T(1024)S(1)}, u32[]{:S(2)}) copy-start(f32[768]{0:T(1024)S(1)} %get-tuple-element.136) | copy-start | bytes 9220
  81.4 99.6 %all-gather.13.cloned.1.call-start = ((), (), s32[]{:S(2)}) async-start(), calls=%async_computation.22 | async-start | bytes 2228224 | tf_op jit(solution)/shard_map/all_gather | solution.py:46
  82.2 163.9 %all-gather.15.cloned.1.call-start = ((), (), s32[]{:S(2)}) async-start(), calls=%async_computation.23 | async-start | bytes 6488064 | tf_op jit(solution)/shard_map/all_gather | solution.py:32
  83.6 11.1 %all-to-all-start = ((s32[16,2,1,128]{3,2,1,0:T(1,128)}), s32[16,2,1,128]{3,2,1,0:T(1,128)S(1)}, u32[]{:S(2)}, u32[]{:S(2)}) async-start(s32[16,2,1,128]{3,2,1,0:T(1,128)} %broadcast_in_dim.307), calls=%async_computation | async-start | bytes 32768 | tf_op jit(solution)/shard_map/all_to_all | solution.py:22
  141.3 50.7 %all-to-all-start.3 = ((bf16[4,128,1024]{2,1,0:T(8,128)(2,1)}), bf16[4,128,1024]{2,1,0:T(8,128)(2,1)S(1)}, u32[]{:S(2)}, u32[]{:S(2)}) async-start(bf16[4,128,1024]{2,1,0:T(8,128)(2,1)} %broadcast_in_dim.313), calls=%async_computation.3 | async-start | bytes 2097152 | tf_op jit(solution)/shard_map/all_to_all | solution.py:22
  193.1 20.1 %all-to-all-start.1 = ((bf16[4,128,1024]{2,1,0:T(8,128)(2,1)}), bf16[4,128,1024]{2,1,0:T(8,128)(2,1)}, u32[]{:S(2)}, u32[]{:S(2)}) async-start(bf16[4,128,1024]{2,1,0:T(8,128)(2,1)} %broadcast_in_dim.310), calls=%async_computation.1 | async-start | bytes 2097152 | tf_op jit(solution)/shard_map/all_to_all | solution.py:22
  197.5 147.5 %all-gather.21.cloned.1.call-start = ((), (), s32[]{:S(2)}) async-start(), calls=%async_computation.26 | async-start | bytes 2228224 | tf_op jit(solution)/shard_map/all_gather | solution.py:46
  267.3 107.3 %all-gather.27.cloned.1.call-start = ((), (), s32[]{:S(2)}) async-start(), calls=%async_computation.29 | async-start | bytes 2228224 | tf_op jit(solution)/shard_map/all_gather | solution.py:46
  273.1 144.2 %all-gather.17.cloned.1.call-start = ((), (), s32[]{:S(2)}) async-start(), calls=%async_computation.24 | async-start | bytes 2228224 | tf_op jit(solution)/shard_map/all_gather | solution.py:46
  299.2 21.5 %all-to-all-start.10 = ((bf16[4,128,1024]{2,1,0:T(8,128)(2,1)}), bf16[4,128,1024]{2,1,0:T(8,128)(2,1)}, u32[]{:S(2)}, u32[]{:S(2)}) async-start(bf16[4,128,1024]{2,1,0:T(8,128)(2,1)} %broadcast_in_dim.343), calls=%async_computation.10 | async-start | bytes 2097152 | tf_op jit(solution)/shard_map/all_to_all | solution.py:22
  322.7 19.8 %all-to-all-start.6 = ((bf16[4,128,1024]{2,1,0:T(8,128)(2,1)}), bf16[4,128,1024]{2,1,0:T(8,128)(2,1)}, u32[]{:S(2)}, u32[]{:S(2)}) async-start(bf16[4,128,1024]{2,1,0:T(8,128)(2,1)} %broadcast_in_dim.322), calls=%async_computation.6 | async-start | bytes 2097152 | tf_op jit(solution)/shard_map/all_to_all | solution.py:22
  327.5 141.0 %all-gather.23.cloned.1.call-start = ((), (), s32[]{:S(2)}) async-start(), calls=%async_computation.27 | async-start | bytes 2228224 | tf_op jit(solution)/shard_map/all_gather | solution.py:46
  490.6 20.3 %all-to-all-start.9 = ((bf16[4,128,1024]{2,1,0:T(8,128)(2,1)}), bf16[4,128,1024]{2,1,0:T(8,128)(2,1)}, u32[]{:S(2)}, u32[]{:S(2)}) async-start(bf16[4,128,1024]{2,1,0:T(8,128)(2,1)} %broadcast_in_dim.339), calls=%async_computation.9 | async-start | bytes 2097152 | tf_op jit(solution)/shard_map/all_to_all | solution.py:22
  512.9 19.2 %all-to-all-start.5 = ((bf16[4,128,1024]{2,1,0:T(8,128)(2,1)}), bf16[4,128,1024]{2,1,0:T(8,128)(2,1)}, u32[]{:S(2)}, u32[]{:S(2)}) async-start(bf16[4,128,1024]{2,1,0:T(8,128)(2,1)} %broadcast_in_dim.318), calls=%async_computation.5 | async-start | bytes 2097152 | tf_op jit(solution)/shard_map/all_to_all | solution.py:22
  517.2 195.6 %all-gather.29.cloned.1.call-start = ((), (), s32[]{:S(2)}) async-start(), calls=%async_computation.30 | async-start | bytes 2228224 | tf_op jit(solution)/shard_map/all_gather | solution.py:46
  555.8 131.9 %all-to-all-start.12 = ((bf16[4,128,1024]{2,1,0:T(8,128)(2,1)}), bf16[4,128,1024]{2,1,0:T(8,128)(2,1)}, u32[]{:S(2)}, u32[]{:S(2)}) async-start(bf16[4,128,1024]{2,1,0:T(8,128)(2,1)} %broadcast_in_dim.354), calls=%async_computation.12 | async-start | bytes 2097152 | tf_op jit(solution)/shard_map/all_to_all | solution.py:22
  560.0 161.9 %all-gather.25.cloned.1.call-start = ((), (), s32[]{:S(2)}) async-start(), calls=%async_computation.28 | async-start | bytes 2228224 | tf_op jit(solution)/shard_map/all_gather | solution.py:46
  689.7 20.5 %all-to-all-start.8 = ((bf16[4,128,1024]{2,1,0:T(8,128)(2,1)}), bf16[4,128,1024]{2,1,0:T(8,128)(2,1)}, u32[]{:S(2)}, u32[]{:S(2)}) async-start(bf16[4,128,1024]{2,1,0:T(8,128)(2,1)} %broadcast_in_dim.333), calls=%async_computation.8 | async-start | bytes 2097152 | tf_op jit(solution)/shard_map/all_to_all | solution.py:22
  740.9 18.3 %all-to-all-start.11 = ((bf16[4,128,1024]{2,1,0:T(8,128)(2,1)}), bf16[4,128,1024]{2,1,0:T(8,128)(2,1)S(1)}, u32[]{:S(2)}, u32[]{:S(2)}) async-start(bf16[4,128,1024]{2,1,0:T(8,128)(2,1)} %broadcast_in_dim.350), calls=%async_computation.11 | async-start | bytes 2097152 | tf_op jit(solution)/shard_map/all_to_all | solution.py:22
  761.3 18.2 %all-to-all-start.7 = ((bf16[4,128,1024]{2,1,0:T(8,128)(2,1)}), bf16[4,128,1024]{2,1,0:T(8,128)(2,1)}, u32[]{:S(2)}, u32[]{:S(2)}) async-start(bf16[4,128,1024]{2,1,0:T(8,128)(2,1)} %broadcast_in_dim.329), calls=%async_computation.7 | async-start | bytes 2097152 | tf_op jit(solution)/shard_map/all_to_all | solution.py:22
  765.6 231.9 %reduce-scatter.2.cloned.1.call-start = ((), (), s32[]{:S(2)}) async-start(), calls=%async_computation.31 | async-start | bytes 12976128 | tf_op jit(solution)/shard_map/reduce_scatter | solution.py:64
  846.2 16.4 %all-to-all-start.4 = ((bf16[4,128,1024]{2,1,0:T(8,128)(2,1)}), bf16[4,128,1024]{2,1,0:T(8,128)(2,1)S(1)}, u32[]{:S(2)}, u32[]{:S(2)}) async-start(bf16[4,128,1024]{2,1,0:T(8,128)(2,1)} %broadcast_in_dim.314), calls=%async_computation.4 | async-start | bytes 2097152 | tf_op jit(solution)/shard_map/all_to_all | solution.py:22
  863.8 16.2 %all-to-all-start.2 = ((bf16[4,128,1024]{2,1,0:T(8,128)(2,1)}), bf16[4,128,1024]{2,1,0:T(8,128)(2,1)}, u32[]{:S(2)}, u32[]{:S(2)}) async-start(bf16[4,128,1024]{2,1,0:T(8,128)(2,1)} %broadcast_in_dim.311), calls=%async_computation.2 | async-start | bytes 2097152 | tf_op jit(solution)/shard_map/all_to_all | solution.py:22
  880.7 12.8 %all-to-all-start.18 = ((bf16[32,2,1024]{2,1,0:T(2,128)(2,1)}), bf16[32,2,1024]{2,1,0:T(2,128)(2,1)S(1)}, u32[]{:S(2)}, u32[]{:S(2)}) async-start(bf16[32,2,1024]{2,1,0:T(2,128)(2,1)} %broadcast_in_dim.363), calls=%async_computation.19 | async-start | bytes 262144 | tf_op jit(solution)/shard_map/all_to_all | solution.py:22
  894.2 11.5 %all-to-all-start.19 = ((bf16[32,2,1024]{2,1,0:T(2,128)(2,1)}), bf16[32,2,1024]{2,1,0:T(2,128)(2,1)S(1)}, u32[]{:S(2)}, u32[]{:S(2)}) async-start(bf16[32,2,1024]{2,1,0:T(2,128)(2,1)} %broadcast_in_dim.364), calls=%async_computation.20 | async-start | bytes 262144 | tf_op jit(solution)/shard_map/all_to_all | solution.py:22
  907.1 13.2 %all-to-all-start.16 = ((bf16[32,2,1024]{2,1,0:T(2,128)(2,1)}), bf16[32,2,1024]{2,1,0:T(2,128)(2,1)S(1)}, u32[]{:S(2)}, u32[]{:S(2)}) async-start(bf16[32,2,1024]{2,1,0:T(2,128)(2,1)} %broadcast_in_dim.361), calls=%async_computation.16 | async-start | bytes 262144 | tf_op jit(solution)/shard_map/all_to_all | solution.py:22
  921.0 11.3 %all-to-all-start.17 = ((bf16[32,2,768]{2,1,0:T(2,128)(2,1)}), bf16[32,2,768]{2,1,0:T(2,128)(2,1)S(1)}, u32[]{:S(2)}, u32[]{:S(2)}) async-start(bf16[32,2,768]{2,1,0:T(2,128)(2,1)} %broadcast_in_dim.362), calls=%async_computation.18 | async-start | bytes 196608 | tf_op jit(solution)/shard_map/all_to_all | solution.py:22
  933.7 12.4 %all-to-all-start.15 = ((bf16[32,2,1024]{2,1,0:T(2,128)(2,1)}), bf16[32,2,1024]{2,1,0:T(2,128)(2,1)S(1)}, u32[]{:S(2)}, u32[]{:S(2)}) async-start(bf16[32,2,1024]{2,1,0:T(2,128)(2,1)} %broadcast_in_dim.360), calls=%async_computation.15 | async-start | bytes 262144 | tf_op jit(solution)/shard_map/all_to_all | solution.py:22
  946.9 12.0 %all-to-all-start.14 = ((bf16[32,2,1024]{2,1,0:T(2,128)(2,1)}), bf16[32,2,1024]{2,1,0:T(2,128)(2,1)S(1)}, u32[]{:S(2)}, u32[]{:S(2)}) async-start(bf16[32,2,1024]{2,1,0:T(2,128)(2,1)} %broadcast_in_dim.359), calls=%async_computation.14 | async-start | bytes 262144 | tf_op jit(solution)/shard_map/all_to_all | solution.py:22
  959.6 11.8 %all-to-all-start.13 = ((bf16[32,2,1024]{2,1,0:T(2,128)(2,1)}), bf16[32,2,1024]{2,1,0:T(2,128)(2,1)S(1)}, u32[]{:S(2)}, u32[]{:S(2)}) async-start(bf16[32,2,1024]{2,1,0:T(2,128)(2,1)} %broadcast_in_dim.358), calls=%async_computation.13 | async-start | bytes 262144 | tf_op jit(solution)/shard_map/all_to_all | solution.py:22
  (236 other events, 3623.9 us)
Sparse Core Ops, SparseCore 0:
  11.5 64.7 all-gather.10
  81.6 48.1 all-gather.18
  132.7 48.2 all-gather.12
  183.1 63.0 all-gather.14
  267.4 48.2 all-gather.20
  317.8 48.2 all-gather.26
  368.9 48.3 all-gather.16
  420.2 48.3 all-gather.22
  544.1 46.2 all-gather.28
  593.1 48.2 all-gather.24
  839.8 157.6 reduce-scatter.1
where the time goes:
time: 1020 us; the launch traced here: 1010 us
  waiting for transfers between devices  341 us (33%)
  matrix products  185 us (18%)
  local copies, waits for them, and re-layouts  154 us (15%)
  other arithmetic  122 us (12%)
  starting transfers between devices  99.9 us (10%)
  blocking collectives  91 us (9%)
  between operations  18 us (2%)
    all_gather x8, waiting for transfers between devices, in_one_piece(): lax.all_gather(both, axis, axis=dim, tiled=True)  114 us
    all_to_all x20, waiting for transfers between devices, copy_for_each(): return lax.all_to_all(copies, axis, split_axis=0, concat_axis=0, tiled=True)  113 us
    all_to_all x20, starting transfers between devices, copy_for_each(): return lax.all_to_all(copies, axis, split_axis=0, concat_axis=0, tiled=True)  99.1 us
    all_gather x4, blocking collectives, in_one_piece(): lax.all_gather(both, axis, axis=dim, tiled=True)  91 us
    all_gather x2, waiting for transfers between devices, gather_turned(): lax.all_gather(both, axis, axis=0, tiled=True)  88 us
    reduce_sum x12, other arithmetic, layer_norm(): return centred * lax.rsqrt(spread + 1e-05) * gain + shift  28 us
    unnamed x479, local copies, waits for them, and re-layouts  27.1 us
    reshape x2, local copies, waits for them, and re-layouts, sum_packed(): lines = jnp.concatenate([b.reshape(length, -1) for b in parts], axis=1)  27 us
  transfers between devices with their start and end apart: 31, of which 24 were waited for; matrix products, arithmetic and copies ran while one was open for 29% of the time, Pallas kernels for 0%

commit v1 on v0

v1 whole, which is shorter than its diff:
```python
import functools

import jax
import jax.numpy as jnp
from jax import lax
from jax.experimental import pallas as pl
from jax.experimental.pallas import tpu as pltpu
from jax.sharding import PartitionSpec as P

HEAD = 64
ROT = 16
LAYERS = 2
MASKED = -1000000000.0
MESH = pl.DeviceIdType.MESH
F32, BF16 = jnp.float32, jnp.bfloat16
VLIM = 56 * 1024 * 1024


def dot(a, b, ca, cb):
    return lax.dot_general(a, b, (((ca,), (cb,)), ((), ())), preferred_element_type=F32)


def places():
    s = lax.axis_index("seq")
    return s, s // 2, lax.rem(s, 2)


def greet(peers):
    barrier = pltpu.get_barrier_semaphore()
    for peer in peers:
        pl.semaphore_signal(barrier, inc=1, device_id=peer, device_id_type=MESH)
    pl.semaphore_wait(barrier, len(peers))


def remote(src, dst, send, recv, peer):
    return pltpu.make_async_remote_copy(
        src_ref=src, dst_ref=dst, send_sem=send, recv_sem=recv, device_id=peer, device_id_type=MESH
    )


def chip_peers():
    _, c, k = places()
    return [{"seq": lax.rem(c + d, 8) * 2 + k} for d in range(1, 8)]


def comm_call(body, out_shape, scratch, ident, in_space, out_space, n_in, name):
    single = not isinstance(out_shape, (tuple, list))
    return pl.pallas_call(
        body,
        out_shape=out_shape,
        in_specs=[pl.BlockSpec(memory_space=in_space)] * n_in,
        out_specs=pl.BlockSpec(memory_space=out_space)
        if single
        else [pl.BlockSpec(memory_space=out_space)] * len(out_shape),
        scratch_shapes=scratch,
        compiler_params=pltpu.CompilerParams(
            collective_id=ident, has_side_effects=True, vmem_limit_bytes=VLIM
        ),
        name=name,
    )


def gather_kernel(src, out, ssem, rsem, fs, fr, lsem):
    b = lax.axis_index("batch")
    s, c, k = places()
    p = b * 8 + c
    partner = {"seq": s + 1 - 2 * k}
    others = []
    for d in range(1, 16):
        p2 = lax.rem(p + d, 16)
        others.append({"batch": p2 // 8, "seq": lax.rem(p2, 8) * 2 + k})
    greet(others + [partner])
    mine = b * 16 + s
    local = pltpu.make_async_copy(src, out.at[mine], lsem)
    local.start()
    copies = [
        remote(src, out.at[mine], ssem.at[d], rsem.at[d], peer) for d, peer in enumerate(others)
    ]
    for copy in copies:
        copy.start()
    onward = [remote(src, out.at[mine], fs.at[0], fr.at[0], partner)]
    onward[0].start()
    for d in range(1, 16):
        copies[d - 1].wait_recv()
        p2 = lax.rem(p - d + 16, 16)
        at = out.at[(p2 // 8) * 16 + lax.rem(p2, 8) * 2 + k]
        copy = remote(at, at, fs.at[d], fr.at[d], partner)
        copy.start()
        onward.append(copy)
    local.wait()
    for copy in copies:
        copy.wait_send()
    for copy in onward:
        copy.wait()


def gather_weights(shard):
    rows, cols = shard.shape
    dma = pltpu.SemaphoreType.DMA
    return comm_call(
        gather_kernel,
        jax.ShapeDtypeStruct((32, rows, cols), shard.dtype),
        [dma((15,)), dma((15,)), dma((16,)), dma((16,)), dma(())],
        1,
        pl.ANY,
        pl.ANY,
        1,
        "gather_weights",
    )(shard).reshape(32 * rows, cols)


def heads_out_kernel(src, kv_out, q_out, ssem, rsem, fs, fr, lsem):
    s, c, k = places()
    partner = {"seq": s + 1 - 2 * k}
    others = chip_peers()
    greet(others + [partner])
    copies = []
    for d, peer in enumerate(others):
        c2 = lax.rem(c + d + 1, 8)
        copies.append(
            remote(src.at[c2, 0], kv_out.at[s], ssem.at[0, d], rsem.at[0, d], peer)
        )
        copies[-1].start()
    copies_q = []
    for d, peer in enumerate(others):
        c2 = lax.rem(c + d + 1, 8)
        copies_q.append(
            remote(src.at[c2, 1], q_out.at[c], ssem.at[1, d], rsem.at[1, d], peer)
        )
        copies_q[-1].start()
    onward = [remote(src.at[c, 0], kv_out.at[s], fs.at[0], fr.at[0], partner)]
    onward[0].start()
    own_kv = pltpu.make_async_copy(src.at[c, 0], kv_out.at[s], lsem.at[0])
    own_q = pltpu.make_async_copy(src.at[c, 1], q_out.at[c], lsem.at[1])
    own_kv.start()
    own_q.start()
    for d in range(1, 8):
        copies[d - 1].wait_recv()
        at = kv_out.at[lax.rem(c - d + 8, 8) * 2 + k]
        copy = remote(at, at, fs.at[d], fr.at[d], partner)
        copy.start()
        onward.append(copy)
    own_kv.wait()
    own_q.wait()
    for copy in copies:
        copy.wait_send()
    for copy in copies_q:
        copy.wait()
    for copy in onward:
        copy.wait()


def heads_out(qkv):
    dma = pltpu.SemaphoreType.DMA
    return comm_call(
        heads_out_kernel,
        (
            jax.ShapeDtypeStruct((16, 128, 128), BF16),
            jax.ShapeDtypeStruct((8, 128, 128), BF16),
        ),
        [dma((2, 7)), dma((2, 7)), dma((8,)), dma((8,)), dma((2,))],
        2,
        pl.ANY,
        pl.ANY,
        1,
        "heads_out",
    )(qkv)


def swap_kernel(src, out, ssem, rsem, lsem):
    _, c, _ = places()
    others = chip_peers()
    greet(others)
    copies = []
    for d, peer in enumerate(others):
        c2 = lax.rem(c + d + 1, 8)
        copies.append(remote(src.at[c2], out.at[c], ssem.at[d], rsem.at[d], peer))
        copies[-1].start()
    own = pltpu.make_async_copy(src.at[c], out.at[c], lsem)
    own.start()
    own.wait()
    for copy in copies:
        copy.wait()


def swap_chips(blocks):
    dma = pltpu.SemaphoreType.DMA
    return comm_call(
        swap_kernel,
        jax.ShapeDtypeStruct(blocks.shape, blocks.dtype),
        [dma((7,)), dma((7,)), dma(())],
        3,
        pl.ANY,
        pl.ANY,
        1,
        "swap_chips",
    )(blocks)


def heads_back_kernel(dq, dkv, dq_out, dkv_out, other, total, ssem, rsem, psem, lsem):
    s, c, k = places()
    partner = {"seq": s + 1 - 2 * k}
    others = chip_peers()
    greet(others + [partner])
    theirs = remote(dkv.at[1 - k], other, psem.at[0], psem.at[1], partner)
    theirs.start()
    copies = []
    for d, peer in enumerate(others):
        c2 = lax.rem(c + d + 1, 8)
        copies.append(remote(dq.at[c2], dq_out.at[c], ssem.at[0, d], rsem.at[0, d], peer))
        copies[-1].start()
    own_q = pltpu.make_async_copy(dq.at[c], dq_out.at[c], lsem)
    own_q.start()
    theirs.wait()
    total[...] = (dkv[k] + other[...]).astype(BF16)
    for d, peer in enumerate(others):
        c2 = lax.rem(c + d + 1, 8)
        copies.append(
            remote(total.at[c2], dkv_out.at[c], ssem.at[1, d], rsem.at[1, d], peer)
        )
        copies[-1].start()
    own_q.wait()
    own_kv = pltpu.make_async_copy(total.at[c], dkv_out.at[c], lsem)
    own_kv.start()
    own_kv.wait()
    for copy in copies:
        copy.wait()


def heads_back(dq, dkv):
    dma = pltpu.SemaphoreType.DMA
    shape = jax.ShapeDtypeStruct((8, 128, 128), BF16)
    return comm_call(
        heads_back_kernel,
        (shape, shape),
        [
            pltpu.VMEM((8, 128, 128), F32),
            pltpu.VMEM((8, 128, 128), BF16),
            dma((2, 7)),
            dma((2, 7)),
            dma((2,)),
            dma(()),
        ],
        4,
        pltpu.VMEM,
        pltpu.VMEM,
        2,
        "heads_back",
    )(dq, dkv)


def tensor_sum_kernel(part, out, got, ssem, rsem):
    t = lax.axis_index("tensor")
    peers = [{"tensor": lax.rem(t + d, 4)} for d in range(1, 4)]
    greet(peers)
    copies = []
    for d, peer in enumerate(peers):
        copies.append(
            remote(part.at[lax.rem(t + d + 1, 4)], got.at[d], ssem.at[0, d], rsem.at[0, d], peer)
        )
        copies[-1].start()
    for copy in copies:
        copy.wait_recv()
    total = part[t].astype(F32) + got[0].astype(F32) + got[1].astype(F32) + got[2].astype(F32)
    out[t] = total.astype(BF16)
    for d, peer in enumerate(peers):
        copies.append(remote(out.at[t], out.at[t], ssem.at[1, d], rsem.at[1, d], peer))
        copies[-1].start()
    for copy in copies[:3]:
        copy.wait_send()
    for copy in copies[3:]:
        copy.wait()


def tensor_sum(part):
    dma = pltpu.SemaphoreType.DMA
    return comm_call(
        tensor_sum_kernel,
        jax.ShapeDtypeStruct(part.shape, BF16),
        [pltpu.VMEM((3, *part.shape[1:]), BF16), dma((2, 3)), dma((2, 3))],
        5,
        pltpu.VMEM,
        pltpu.VMEM,
        1,
        "tensor_sum",
    )(part)


def scatter_kernel(count, *refs):
    ins, outs = refs[:count], refs[count : 2 * count]
    rest = refs[2 * count :]
    pair, sums, got = rest[:count], rest[count : 2 * count], rest[2 * count : 3 * count]
    ps, pr, ssem, rsem = rest[3 * count :]
    b = lax.axis_index("batch")
    s, c, k = places()
    p = b * 8 + c
    partner = {"seq": s + 1 - 2 * k}
    others = []
    for d in range(1, 16):
        p2 = lax.rem(p + d, 16)
        others.append({"batch": p2 // 8, "seq": lax.rem(p2, 8) * 2 + k})
    greet(others + [partner])
    first = []
    for d in range(16):
        p2 = lax.rem(p + d + 1, 16)
        for a in range(count):
            copy = remote(
                ins[a].at[p2, 1 - k], pair[a].at[p2], ps.at[a, d], pr.at[a, d], partner
            )
            copy.start()
            first.append(copy)
    second = []
    for d in range(16):
        p2 = lax.rem(p + d + 1, 16)
        for a in range(count):
            first[d * count + a].wait_recv()
            total = ins[a][p2, k].astype(F32) + pair[a][p2].astype(F32)
            if d < 15:
                sums[a][d] = total.astype(BF16)
                copy = remote(sums[a].at[d], got[a].at[d], ssem.at[a, d], rsem.at[a, d], others[d])
                copy.start()
                second.append(copy)
            else:
                outs[a][...] = total
    for d in range(15):
        for a in range(count):
            second[d * count + a].wait_recv()
            outs[a][...] += got[a][d].astype(F32)
    for copy in first:
        copy.wait_send()
    for copy in second:
        copy.wait_send()


def scatter_sum(arrays):
    count = len(arrays)
    dma = pltpu.SemaphoreType.DMA
    shaped = [a.reshape(16, 2, 32, a.shape[1]) for a in arrays]
    widths = [a.shape[1] for a in arrays]
    return comm_call(
        functools.partial(scatter_kernel, count),
        tuple(jax.ShapeDtypeStruct((32, w), F32) for w in widths),
        [pltpu.VMEM((16, 32, w), BF16) for w in widths]
        + [pltpu.VMEM((15, 32, w), BF16) for w in widths]
        + [pltpu.VMEM((15, 32, w), BF16) for w in widths]
        + [dma((count, 16)), dma((count, 16)), dma((count, 15)), dma((count, 15))],
        6,
        pltpu.VMEM,
        pltpu.VMEM,
        count,
        "scatter_sum",
    )(*shaped)


def turned(values, cosine, sine):
    lane = lax.broadcasted_iota(jnp.int32, values.shape, 1)
    swapped = jnp.where(
        lane < 8, pltpu.roll(values, 120, axis=1), pltpu.roll(values, 8, axis=1)
    )
    return values * cosine + swapped * sine


def normal(values):
    centred = values - jnp.mean(values, axis=-1, keepdims=True)
    rstd = lax.rsqrt(jnp.mean(centred * centred, axis=-1, keepdims=True) + 1e-05)
    return centred * rstd, rstd


def project_kernel(x, g1, b1, g2, b2, bias, weight, cosine, sine, h1, h2, qkv):
    hat, _ = normal(x[...])
    h1[...] = (hat * g1[...] + b1[...]).astype(BF16)
    h2[...] = (hat * g2[...] + b2[...]).astype(BF16)
    proj = dot(h1[...], weight[...], 1, 0) + bias[...]
    cos, sin = cosine[...], sine[...]
    lane = lax.broadcasted_iota(jnp.int32, (128, 128), 1)
    for m in range(2):
        rows = proj[m * 128 : (m + 1) * 128]
        for h in range(4):
            pair = rows[:, 128 * h : 128 * (h + 1)]
            qkv[m * 4 + h, 0] = turned(pair, cos, sin).astype(BF16)
            q = rows[:, 512 + 128 * (h // 2) : 640 + 128 * (h // 2)]
            if h % 2:
                q = pltpu.roll(q, 64, axis=1)
            q = turned(q, cos, sin) * 0.125
            qkv[m * 4 + h, 1] = jnp.where(lane < 64, q, 0.0).astype(BF16)


def local_call(body, out_shape, in_specs, name, scratch=()):
    return pl.pallas_call(
        body,
        out_shape=out_shape,
        grid=(1,),
        in_specs=in_specs,
        out_specs=jax.tree.map(lambda o: whole(o.shape), out_shape),
        scratch_shapes=scratch,
        compiler_params=pltpu.CompilerParams(vmem_limit_bytes=VLIM),
        name=name,
    )


def whole(shape):
    return pl.BlockSpec(shape, lambda i: (0,) * len(shape))


def columns(width, at):
    return pl.BlockSpec((1024, width), lambda i: (0, at))


def wholes(*arrays):
    return [whole(a.shape) for a in arrays]


def project(x, g1, b1, g2, b2, bias, gathered, cosine, sine):
    sds = jax.ShapeDtypeStruct
    return local_call(
        project_kernel,
        (
            sds((256, 1024), BF16),
            sds((256, 1024), BF16),
            sds((8, 2, 128, 128), BF16),
        ),
        wholes(x, g1, b1, g2, b2, bias) + [columns(768, 0)] + wholes(cosine, sine),
        "project",
    )(x, g1, b1, g2, b2, bias, gathered, cosine, sine)


def scores_of(q, keys, low, high):
    s = dot(q, keys, 1, 1)
    place = lax.broadcasted_iota(jnp.int32, s.shape, 1)
    return jnp.where((place >= low) & (place <= high), s, MASKED)


def attend_kernel(kv, q, low, high, ctx, lse):
    for i in range(8):
        n = 256 * (i + 1)
        keys = kv[0 : 2 * (i + 1)].reshape(n, 128)
        s = scores_of(q[i], keys, low[i], high[i])
        top = jnp.max(s, axis=-1, keepdims=True)
        e = jnp.exp(s - top)
        total = jnp.sum(e, axis=-1, keepdims=True)
        soft = (e * (1.0 / total)).astype(BF16)
        ctx[i] = dot(soft, keys, 1, 0).astype(BF16)
        lse[i] = top + jnp.log(total)


def attend(kv, q, low, high):
    sds = jax.ShapeDtypeStruct
    return local_call(
        attend_kernel,
        (sds((8, 128, 128), BF16), sds((8, 128, 1), F32)),
        wholes(kv, q, low, high),
        "attend",
    )(kv, q, low, high)


def attend_back_kernel(kv, q, dctx, lse, low, high, dq, dkv, total):
    for i in reversed(range(8)):
        n = 256 * (i + 1)
        keys = kv[0 : 2 * (i + 1)].reshape(n, 128)
        s = scores_of(q[i], keys, low[i], high[i])
        soft = jnp.exp(s - lse[i])
        dsoft = dot(dctx[i], keys, 1, 1)
        term = jnp.sum(soft * dsoft, axis=-1, keepdims=True)
        ds = (soft * (dsoft - term)).astype(BF16)
        dq[i] = (dot(ds, keys, 1, 0) * 0.125).astype(BF16)
        both = jnp.concatenate([ds, soft.astype(BF16)], axis=0)
        right = jnp.concatenate([q[i], dctx[i]], axis=0)
        fresh = dot(both, right, 0, 0)
        if i == 7:
            total[...] = fresh
        else:
            total[0:n] += fresh
    for i in range(8):
        dkv[0, i] = total[256 * i : 256 * i + 128]
        dkv[1, i] = total[256 * i + 128 : 256 * i + 256]


def attend_back(kv, q, dctx, lse, low, high):
    sds = jax.ShapeDtypeStruct
    return local_call(
        attend_back_kernel,
        (sds((8, 128, 128), BF16), sds((2, 8, 128, 128), F32)),
        wholes(kv, q, dctx, lse, low, high),
        "attend_back",
        [pltpu.VMEM((2048, 128), F32)],
    )(kv, q, dctx, lse, low, high)


def in_quarters(value, ref):
    for t in range(4):
        ref[t] = value[:, 256 * t : 256 * (t + 1)].astype(BF16)


def feed_kernel(ctx_in, h2, dense, expand, shrink, bias, u, act, ctx, part):
    lane = lax.broadcasted_iota(jnp.int32, (128, 128), 1)
    for m in range(2):
        for h in range(2):
            left = pltpu.roll(ctx_in[m * 4 + 2 * h].astype(F32), 64, axis=1)
            right = ctx_in[m * 4 + 2 * h + 1].astype(F32)
            ctx[m * 128 : (m + 1) * 128, 128 * h : 128 * (h + 1)] = jnp.where(
                lane < 64, left, right
            ).astype(BF16)
    inner = dot(h2[...], expand[...], 1, 0) + bias[...]
    u[...] = inner
    act[...] = (0.5 * inner * (1.0 + lax.erf(inner * 0.7071067811865476))).astype(BF16)
    in_quarters(dot(ctx[...], dense[...], 1, 1) + dot(act[...], shrink[...], 1, 1), part)


def feed(ctx_in, h2, gathered, bias):
    sds = jax.ShapeDtypeStruct
    return local_call(
        feed_kernel,
        (
            sds((256, 1024), F32),
            sds((256, 1024), BF16),
            sds((256, 256), BF16),
            sds((4, 256, 256), BF16),
        ),
        wholes(ctx_in, h2) + [columns(256, 3), columns(1024, 1), columns(1024, 2)] + wholes(bias),
        "feed",
    )(ctx_in, h2, gathered, gathered, gathered, bias)


def feed_back_kernel(
    grad, x, g2, u, act, ctx, h2, dense, expand, shrink, dctx, wgrad, z2, small
):
    gb = grad[...].astype(BF16)
    dact = dot(gb, shrink[...], 1, 0)
    inner = u[...]
    slope = 0.5 * (1.0 + lax.erf(inner * 0.7071067811865476)) + inner * (
        0.3989422804014327 * jnp.exp(-0.5 * inner * inner)
    )
    du = (dact * slope).astype(BF16)
    dc = dot(gb, dense[...], 1, 0)
    lane = lax.broadcasted_iota(jnp.int32, (128, 128), 1)
    for m in range(2):
        for h in range(4):
            piece = dc[m * 128 : (m + 1) * 128, 128 * (h // 2) : 128 * (h // 2 + 1)]
            if h % 2 == 0:
                piece = pltpu.roll(piece, 64, axis=1)
            dctx[m * 4 + h] = jnp.where(lane >= 64, piece, 0.0).astype(BF16)
    wgrad[:, 0:256] = dot(gb, ctx[...], 0, 0).astype(BF16)
    wgrad[:, 256:1280] = dot(h2[...], du, 0, 0).astype(BF16)
    wgrad[:, 1280:2304] = dot(gb, act[...], 0, 0).astype(BF16)
    dh2 = dot(du, expand[...], 1, 1)
    hat, _ = normal(x[...])
    z2[...] = dh2 * g2[...]
    small[0:1] = jnp.sum(dh2 * hat, axis=0, keepdims=True)
    small[1:2] = jnp.sum(dh2, axis=0, keepdims=True)
    small[2:3] = jnp.sum(gb.astype(F32), axis=0, keepdims=True)
    small[3:4] = jnp.sum(du.astype(F32), axis=0, keepdims=True)


def feed_back(grad, x, g2, u, act, ctx, h2, gathered):
    sds = jax.ShapeDtypeStruct
    return local_call(
        feed_back_kernel,
        (
            sds((8, 128, 128), BF16),
            sds((1024, 2304), BF16),
            sds((256, 1024), F32),
            sds((4, 1024), F32),
        ),
        wholes(grad, x, g2, u, act, ctx, h2)
        + [columns(256, 3), columns(1024, 1), columns(1024, 2)],
        "feed_back",
    )(grad, x, g2, u, act, ctx, h2, gathered, gathered, gathered)


def project_back_kernel(
    dq, dkv, cosine, sine, h1, weight, z2, x, g1, wgrad, part, small, bias_grad, dproj
):
    cos, sin = cosine[...], -sine[...]
    lane = lax.broadcasted_iota(jnp.int32, (128, 128), 1)
    for m in range(2):
        rows = pl.ds(m * 128, 128)
        for h in range(4):
            dproj[rows, 128 * h : 128 * (h + 1)] = turned(
                dkv[m * 4 + h].astype(F32), cos, sin
            ).astype(BF16)
        for h in range(2):
            left = turned(dq[m * 4 + 2 * h].astype(F32), cos, sin)
            right = turned(dq[m * 4 + 2 * h + 1].astype(F32), cos, sin)
            dproj[rows, 512 + 128 * h : 640 + 128 * h] = jnp.where(
                lane < 64, left, pltpu.roll(right, 64, axis=1)
            ).astype(BF16)
    dp = dproj[...]
    wgrad[...] = dot(h1[...], dp, 0, 0).astype(BF16)
    bias_grad[...] = jnp.sum(dp.astype(F32), axis=0, keepdims=True)
    dh1 = dot(dp, weight[...], 1, 1)
    hat, _ = normal(x[...])
    small[0:1] = jnp.sum(dh1 * hat, axis=0, keepdims=True)
    small[1:2] = jnp.sum(dh1, axis=0, keepdims=True)
    in_quarters(dh1 * g1[...] + z2[...], part)


def project_back(dq, dkv, cosine, sine, h1, gathered, z2, x, g1):
    sds = jax.ShapeDtypeStruct
    return local_call(
        project_back_kernel,
        (
            sds((1024, 768), BF16),
            sds((4, 256, 256), BF16),
            sds((2, 1024), F32),
            sds((1, 768), F32),
        ),
        wholes(dq, dkv, cosine, sine, h1) + [columns(768, 0)] + wholes(z2, x, g1),
        "project_back",
        [pltpu.VMEM((256, 768), BF16)],
    )(dq, dkv, cosine, sine, h1, gathered, z2, x, g1)


def head_order(value):
    lead = value.shape[:-1]
    parts = value.reshape(*lead, 4, 3, HEAD)
    keys = parts[..., 1:3, :].reshape(*lead, 512)
    return jnp.concatenate([keys, parts[..., 0, :].reshape(*lead, 256)], axis=-1)


def head_order_back(value):
    lead = value.shape[:-1]
    keys = value[..., :512].reshape(*lead, 4, 2, HEAD)
    queries = value[..., 512:].reshape(*lead, 4, 1, HEAD)
    return jnp.concatenate([queries, keys], axis=-2).reshape(*lead, 768)


def from_quarters(value):
    return value.transpose(1, 0, 2).reshape(256, 1024).astype(F32)


def local(
    hidden_in,
    document_ids,
    first_gain,
    first_shift,
    second_gain,
    second_shift,
    attn_weight,
    attn_bias,
    dense_weight,
    dense_bias,
    expand_weight,
    expand_bias,
    shrink_weight,
    shrink_bias,
    output_grad,
):
    seq_at = lax.axis_index("seq")
    chip, core = seq_at // 2, lax.rem(seq_at, 2)
    unit_micro = chip // 4
    lead = jnp.arange(ROT // 2, dtype=F32) * 2
    inverse = 10000.0 ** (-lead / ROT)
    place = (seq_at * 128 + jnp.arange(128, dtype=jnp.int32)).astype(F32)
    angles = place[:, None] * inverse[None, :]
    cos, sin = jnp.cos(angles), jnp.sin(angles)
    ones, zeros = jnp.ones((128, 112), F32), jnp.zeros((128, 112), F32)
    cosine = jnp.concatenate([cos, cos, ones], axis=1)
    sine = jnp.concatenate([-sin, sin, zeros], axis=1)

    idents = lax.all_gather(document_ids, "seq", axis=2, tiled=True)
    mine = lax.dynamic_index_in_dim(idents[:, 0], unit_micro, 0, keepdims=False)
    count0 = jnp.sum((mine == 0).astype(jnp.int32))
    count1 = jnp.sum((mine == 1).astype(jnp.int32))
    start = jnp.where(mine == 0, 0, jnp.where(mine == 1, count0, count0 + count1))
    high = jnp.arange(2048, dtype=jnp.int32).reshape(8, 2, 128)
    high = lax.dynamic_index_in_dim(high, core, 1, keepdims=False)[..., None]
    low = lax.dynamic_index_in_dim(start.reshape(8, 2, 128), core, 1, keepdims=False)[..., None]

    shards = jnp.concatenate(
        [
            head_order(attn_weight),
            jnp.swapaxes(dense_weight, 1, 2),
            expand_weight,
            jnp.swapaxes(shrink_weight, 1, 2),
        ],
        axis=2,
    )
    weights = [gather_weights(shards[layer]) for layer in range(LAYERS)]
    bias_order = head_order(attn_bias)

    x = hidden_in.reshape(256, 1024)
    kept = []
    for layer in range(LAYERS):
        row = slice(layer, layer + 1)
        h1, h2, qkv = project(
            x,
            first_gain[row],
            first_shift[row],
            second_gain[row],
            second_shift[row],
            bias_order[row],
            weights[layer],
            cosine,
            sine,
        )
        kv, q = heads_out(qkv)
        ctx_out, lse = attend(kv, q, low, high)
        ctx_in = swap_chips(ctx_out)
        u, act, ctx, part = feed(ctx_in, h2, weights[layer], expand_bias[row])
        kept.append((x, h1, h2, kv, q, lse, u, act, ctx))
        x = x + from_quarters(tensor_sum(part)) + dense_bias[row] + shrink_bias[row]
    hidden_out = x.reshape(2, 1, 128, 1024)

    grad = output_grad.reshape(256, 1024)
    wide, narrow, by_all, by_rows = [None] * 2, [None] * 2, [None] * 2, [None] * 2
    for layer in reversed(range(LAYERS)):
        row = slice(layer, layer + 1)
        x, h1, h2, kv, q, lse, u, act, ctx = kept[layer]
        dctx, wide[layer], z2, small2 = feed_back(
            grad, x, second_gain[row], u, act, ctx, h2, weights[layer]
        )
        dctx_in = swap_chips(dctx)
        dq, dkv = attend_back(kv, q, dctx_in, lse, low, high)
        dq_in, dkv_in = heads_back(dq, dkv)
        narrow[layer], part, small1, bias_grad = project_back(
            dq_in, dkv_in, cosine, sine, h1, weights[layer], z2, x, first_gain[row]
        )
        z = from_quarters(tensor_sum(part))
        hat, rstd = normal(x)
        grad = grad + rstd * (
            z
            - jnp.mean(z, axis=-1, keepdims=True)
            - hat * jnp.mean(z * hat, axis=-1, keepdims=True)
        )
        by_all[layer] = jnp.concatenate([small1, small2[:2]], axis=0)
        by_rows[layer] = jnp.concatenate([bias_grad[0], small2[2], small2[3]], axis=0)
    input_grad = grad.reshape(2, 1, 128, 1024)

    sums = scatter_sum([narrow[0], narrow[1], wide[0], wide[1]])
    narrow_sum = head_order_back(jnp.stack(sums[:2]))
    wide_sum = jnp.stack(sums[2:])
    norms = lax.psum(jnp.stack(by_all), ("batch", "seq", "tensor"))
    rows = lax.psum(jnp.stack(by_rows), ("batch", "seq"))
    branch_bias = rows[:, 768:1792]
    return (
        hidden_out,
        input_grad,
        norms[:, 0],
        norms[:, 1],
        norms[:, 2],
        norms[:, 3],
        narrow_sum,
        head_order_back(rows[:, :768]),
        jnp.swapaxes(wide_sum[..., :256], 1, 2),
        branch_bias,
        wide_sum[..., 256:1280],
        rows[:, 1792:],
        jnp.swapaxes(wide_sum[..., 1280:], 1, 2),
        branch_bias,
    )


def solution(mesh):
    rows, spread, split = P(None, "batch", "seq", None), P(None, ("batch", "seq"), "tensor"), P(
        None, "tensor"
    )
    across = P(None, "tensor", ("batch", "seq"))
    return jax.shard_map(
        local,
        mesh=mesh,
        in_specs=(
            rows,
            P(None, "batch", "seq"),
            P(),
            P(),
            P(),
            P(),
            spread,
            split,
            across,
            P(),
            spread,
            split,
            across,
            P(),
            rows,
        ),
        out_specs=(
            rows,
            rows,
            P(),
            P(),
            P(),
            P(),
            spread,
            split,
            across,
            P(),
            spread,
            split,
            across,
            P(),
        ),
        check_vma=False,
    )
```

time: 1020 us -> 771 us (0.76)
  Pallas kernels: 0 us -> 477 us
  waiting for transfers between devices: 341 us -> 0 us
  matrix products: 185 us -> 0 us
  blocking collectives: 91 us -> 217 us
  local copies, waits for them, and re-layouts: 154 us -> 36.8 us
  starting transfers between devices: 99.9 us -> 0 us
  other arithmetic: 122 us -> 25.5 us
  between operations: 18 us -> 3.07 us
    pallas_call x0 -> x27, Pallas kernels: none -> 477 us  [the longest x1 121 us: scatter_sum(): comm_call(functools.partial(scatter_kernel, count), tuple((jax.ShapeDtype...]
    all_gather x10 -> x0, waiting for transfers between devices: 202 us -> none  [the longest x8 114 us: in_one_piece(): lax.all_gather(both, axis, axis=dim, tiled=True)]
    psum x0 -> x2, blocking collectives: none -> 194 us  [the longest x1 129 us: local(): rows = lax.psum(jnp.stack(by_rows), ('batch', 'seq'))]
    dot_general x76 -> x0, matrix products: 185 us -> none  [the longest x8 21.6 us: masked_scores(): jnp.einsum('sqhd,skhd->shqk', query_blocks, key_blocks, preferred_element...]
    all_to_all x20 -> x0, waiting for transfers between devices: 113 us -> none  [copy_for_each(): return lax.all_to_all(copies, axis, split_axis=0, concat_axis=0, tiled=True)]
    all_to_all x20 -> x0, starting transfers between devices: 99.1 us -> none  [copy_for_each(): return lax.all_to_all(copies, axis, split_axis=0, concat_axis=0, tiled=True)]
    all_gather x4 -> x1, blocking collectives: 91 us -> 22.6 us  [local(): idents = lax.all_gather(document_ids, 'seq', axis=2, tiled=True)]
    reduce_sum x39 -> x8, other arithmetic: 49.3 us -> 6.02 us  [the longest x2 3.31 us: local(): jnp.mean(z * hat, axis=-1, keepdims=True)]
  transfers between devices with their start and end apart: 31 -> 0, of which waited for: 24 -> 0; matrix products, arithmetic and copies ran while one was open for 29% -> 0% of each run, Pallas kernels for 0% -> 0%
where the time goes in v1:
time: 771 us; the launch traced here: 759 us
  Pallas kernels  477 us (62%)
  blocking collectives  217 us (28%)
  local copies, waits for them, and re-layouts  36.8 us (5%)
  other arithmetic  25.5 us (3%)
    psum x1, blocking collectives, local(): rows = lax.psum(jnp.stack(by_rows), ('batch', 'seq'))  129 us
    pallas_call x1, Pallas kernels, scatter_sum(): comm_call(functools.partial(scatter_kernel, count), tuple((jax.ShapeDtype...  121 us
    pallas_call x2, Pallas kernels, gather_weights(): comm_call(gather_kernel, jax.ShapeDtypeStruct((32, rows, cols), shard.dty...  104 us
    pallas_call x4, Pallas kernels, tensor_sum(): comm_call(tensor_sum_kernel, jax.ShapeDtypeStruct(part.shape, BF16), [plt...  76.1 us
    psum x1, blocking collectives, local(): norms = lax.psum(jnp.stack(by_all), ('batch', 'seq', 'tensor'))  65.7 us
    pallas_call x4, Pallas kernels, swap_chips(): comm_call(swap_kernel, jax.ShapeDtypeStruct(blocks.shape, blocks.dtype),...  35.4 us
    pallas_call x2, Pallas kernels, heads_back(): comm_call(heads_back_kernel, (shape, shape), [pltpu.VMEM((8, 128, 128), F...  28.1 us
    pallas_call x2, Pallas kernels, attend_back(): local_call(attend_back_kernel, (sds((8, 128, 128), BF16), sds((2, 8, 128,...  27.1 us

profile of v1, /device:TPU:24, one launch (start us, length us, event | category | flops | bytes accessed | tf_op | source)
XLA Modules:
  0.0 758.9 jit_solution(2393440042290381227)
XLA Ops:
  0.7 22.6 %all_gather.3 = s32[2,1,2048]{2,1,0:T(1,128)S(1)} all-gather(s32[2,1,128]{2,1,0:T(1,128)} %param.16), channel_id=1, replica_groups=mesh['batch'=2,'seq'=16,'tensor'=4] {'seq'}, dimensions={2}, use_global_device_ids=true | all-gather | bytes 17408 | tf_op jit(solution)/shard_map/all_gather | solution.py:660
  34.6 54.3 %gather_weights.2 = bf16[32,32,3072]{2,1,0:T(8,128)(2,1)} custom-call(bf16[32,3072]{1,0:T(8,128)(2,1)} %get-tuple-element.166.src), custom_call_target="tpu_custom_call" | custom-call | tf_op jit(solution)/shard_map/gather_weights/pallas_call | solution.py:100
  91.1 4.1 project.2
  95.2 13.8 %heads_out.2 = (bf16[16,128,128]{2,1,0:T(8,128)(2,1)}, bf16[8,128,128]{2,1,0:T(8,128)(2,1)}) custom-call(bf16[8,2,128,128]{3,2,1,0:T(8,128)(2,1)} %get-tuple-element.64.src), custom_call_target="tpu_custom_call" | custom-call | tf_op jit(solution)/shard_map/heads_out/pallas_call | solution.py:155
  109.0 6.7 attend.2
  115.7 8.7 %swap_chips.4.ctx_in = bf16[8,128,128]{2,1,0:T(8,128)(2,1)} custom-call(bf16[8,128,128]{2,1,0:T(8,128)(2,1)} %get-tuple-element.67.src), custom_call_target="tpu_custom_call" | custom-call | tf_op jit(solution)/shard_map/swap_chips/pallas_call | solution.py:188
  125.0 5.0 feed.2
  130.0 19.0 %tensor_sum.4 = bf16[4,256,256]{2,1,0:T(8,128)(2,1)} custom-call(bf16[4,256,256]{2,1,0:T(8,128)(2,1)} %get-tuple-element.69.part), custom_call_target="tpu_custom_call" | custom-call | tf_op jit(solution)/shard_map/tensor_sum/pallas_call | solution.py:277
  154.2 49.8 %gather_weights.3 = bf16[32,32,3072]{2,1,0:T(8,128)(2,1)} custom-call(bf16[32,3072]{1,0:T(8,128)(2,1)} %get-tuple-element.165.src), custom_call_target="tpu_custom_call" | custom-call | tf_op jit(solution)/shard_map/gather_weights/pallas_call | solution.py:100
  204.0 4.1 project.3
  208.1 12.5 %heads_out.3 = (bf16[16,128,128]{2,1,0:T(8,128)(2,1)}, bf16[8,128,128]{2,1,0:T(8,128)(2,1)}) custom-call(bf16[8,2,128,128]{3,2,1,0:T(8,128)(2,1)} %get-tuple-element.70.src), custom_call_target="tpu_custom_call" | custom-call | tf_op jit(solution)/shard_map/heads_out/pallas_call | solution.py:155
  220.6 6.7 attend.3
  227.3 8.7 %swap_chips.5.ctx_in = bf16[8,128,128]{2,1,0:T(8,128)(2,1)} custom-call(bf16[8,128,128]{2,1,0:T(8,128)(2,1)} %get-tuple-element.73.src), custom_call_target="tpu_custom_call" | custom-call | tf_op jit(solution)/shard_map/swap_chips/pallas_call | solution.py:188
  236.0 5.0 feed.3
  241.0 8.7 %feed_back.2 = (bf16[8,128,128]{2,1,0:T(8,128)(2,1)}, bf16[1024,2304]{1,0:T(8,128)(2,1)}, f32[256,1024]{1,0:T(8,128)}, f32[4,1024]{1,0:T(4,128)}) custom-call(f32[256,1024]{1,0:T(8,128)} %bitcast.131, f32[256,1024]{1,0:T(8,128)} %add_add_fusion.x, f32[1,1024]{1,0:T(1,128)} %get-tuple-element.216.g2, f32[256,1024]{1,0:T(8,128)} %get-tuple-element.76.u, ...), custom_call_target="tpu_custom_call" | custom-call | tf_op jit(solution)/shard_map/feed_back/pallas_call | solution.py:556
  249.6 8.7 %swap_chips.6.dctx = bf16[8,128,128]{2,1,0:T(8,128)(2,1)} custom-call(bf16[8,128,128]{2,1,0:T(8,128)(2,1)} %get-tuple-element.79.src), custom_call_target="tpu_custom_call" | custom-call | tf_op jit(solution)/shard_map/swap_chips/pallas_call | solution.py:188
  258.4 19.0 %attend_back.2 = (bf16[8,128,128]{2,1,0:T(8,128)(2,1)}, f32[2,8,128,128]{3,2,1,0:T(8,128)}) custom-call(bf16[16,128,128]{2,1,0:T(8,128)(2,1)} %get-tuple-element.71.kv, bf16[8,128,128]{2,1,0:T(8,128)(2,1)} %get-tuple-element.72.q, bf16[8,128,128]{2,1,0:T(8,128)(2,1)} %swap_chips.6.dctx, f32[8,128,1]{2,1,0:T(8,128)} %get-tuple-element.80.lse, ...), custom_call_target="tpu_custom_call" | custom-call | tf_op jit(solution)/shard_map/attend_back/pallas_call | solution.py:480
  277.4 14.0 %heads_back.2 = (bf16[8,128,128]{2,1,0:T(8,128)(2,1)}, bf16[8,128,128]{2,1,0:T(8,128)(2,1)}) custom-call(bf16[8,128,128]{2,1,0:T(8,128)(2,1)} %get-tuple-element.81.dq, f32[2,8,128,128]{3,2,1,0:T(8,128)} %get-tuple-element.82.dkv), custom_call_target="tpu_custom_call" | custom-call | tf_op jit(solution)/shard_map/heads_back/pallas_call | solution.py:233
  291.4 4.9 project_back.2
  296.3 19.4 %tensor_sum.6 = bf16[4,256,256]{2,1,0:T(8,128)(2,1)} custom-call(bf16[4,256,256]{2,1,0:T(8,128)(2,1)} %get-tuple-element.87.part), custom_call_target="tpu_custom_call" | custom-call | tf_op jit(solution)/shard_map/tensor_sum/pallas_call | solution.py:277
  330.1 8.6 %feed_back.3 = (bf16[8,128,128]{2,1,0:T(8,128)(2,1)}, bf16[1024,2304]{1,0:T(8,128)(2,1)}, f32[256,1024]{1,0:T(8,128)}, f32[4,1024]{1,0:T(4,128)}) custom-call(f32[256,1024]{1,0:T(8,128)} %multiply_add_fusion.grad, f32[256,1024]{1,0:T(8,128)} %bitcast.129, f32[1,1024]{1,0:T(1,128)} %get-tuple-element.215.g2, f32[256,1024]{1,0:T(8,128)} %get-tuple-element.88.u, ...), custom_call_target="tpu_custom_call" | custom-call | tf_op jit(solution)/shard_map/feed_back/pallas_call | solution.py:556
  338.7 9.3 %swap_chips.7.dctx = bf16[8,128,128]{2,1,0:T(8,128)(2,1)} custom-call(bf16[8,128,128]{2,1,0:T(8,128)(2,1)} %get-tuple-element.91.src), custom_call_target="tpu_custom_call" | custom-call | tf_op jit(solution)/shard_map/swap_chips/pallas_call | solution.py:188
  348.0 8.1 %attend_back.3 = (bf16[8,128,128]{2,1,0:T(8,128)(2,1)}, f32[2,8,128,128]{3,2,1,0:T(8,128)}) custom-call(bf16[16,128,128]{2,1,0:T(8,128)(2,1)} %get-tuple-element.65.kv, bf16[8,128,128]{2,1,0:T(8,128)(2,1)} %get-tuple-element.66.q, bf16[8,128,128]{2,1,0:T(8,128)(2,1)} %swap_chips.7.dctx, f32[8,128,1]{2,1,0:T(8,128)} %get-tuple-element.92.lse, ...), custom_call_target="tpu_custom_call" | custom-call | tf_op jit(solution)/shard_map/attend_back/pallas_call | solution.py:480
  356.1 14.1 %heads_back.3 = (bf16[8,128,128]{2,1,0:T(8,128)(2,1)}, bf16[8,128,128]{2,1,0:T(8,128)(2,1)}) custom-call(bf16[8,128,128]{2,1,0:T(8,128)(2,1)} %get-tuple-element.93.dq, f32[2,8,128,128]{3,2,1,0:T(8,128)} %get-tuple-element.94.dkv), custom_call_target="tpu_custom_call" | custom-call | tf_op jit(solution)/shard_map/heads_back/pallas_call | solution.py:233
  370.2 4.9 project_back.3
  375.1 120.9 %scatter_sum.1 = (f32[32,768]{1,0:T(8,128)}, f32[32,768]{1,0:T(8,128)}, f32[32,2304]{1,0:T(8,128)}, f32[32,2304]{1,0:T(8,128)}) custom-call(bf16[16,2,32,768]{3,2,1,0:T(8,128)(2,1)} %bitcast.137, bf16[16,2,32,768]{3,2,1,0:T(8,128)(2,1)} %bitcast.136, bf16[16,2,32,2304]{3,2,1,0:T(8,128)(2,1)} %bitcast.133, bf16[16,2,32,2304]{3,2,1,0:T(8,128)(2,1)} %bitcast.132), custom_call_target="tpu_custom_call" | custom-call | tf_op jit(solution)/shard_map/scatter_sum/pallas_call | solution.py:340
  499.6 128.6 %psum.15 = f32[2,2816]{1,0:T(2,128)S(1)} all-reduce(f32[2,2816]{1,0:T(2,128)S(1)} %pad_maximum_fusion.6), channel_id=1, replica_groups=mesh['batch'=2,'seq'=16,'tensor'=4] {'batch','seq'}, use_global_device_ids=true, to_apply=%region_11.12 | all-reduce | flops 5632 | bytes 45056 | tf_op jit(solution)/shard_map/psum | solution.py:733
  633.1 65.7 %psum.14 = f32[2,4,1024]{2,1,0:T(4,128)S(1)} all-reduce(f32[2,4,1024]{2,1,0:T(4,128)S(1)} %pad_maximum_fusion.5), channel_id=1, replica_groups=mesh['batch'=2,'seq'=16,'tensor'=4] {'batch','seq','tensor'}, use_global_device_ids=true, to_apply=%region_10.11 | all-reduce | flops 8192 | bytes 65536 | tf_op jit(solution)/shard_map/psum | solution.py:732
  701.2 19.9 %tensor_sum.7 = bf16[4,256,256]{2,1,0:T(8,128)(2,1)} custom-call(bf16[4,256,256]{2,1,0:T(8,128)(2,1)} %get-tuple-element.99.part), custom_call_target="tpu_custom_call" | custom-call | tf_op jit(solution)/shard_map/tensor_sum/pallas_call | solution.py:277
  727.8 2.9 reshape.483
  730.7 17.8 %tensor_sum.5 = bf16[4,256,256]{2,1,0:T(8,128)(2,1)} custom-call(bf16[4,256,256]{2,1,0:T(8,128)(2,1)} %get-tuple-element.75.part), custom_call_target="tpu_custom_call" | custom-call | tf_op jit(solution)/shard_map/tensor_sum/pallas_call | solution.py:277
  754.1 3.8 fusion.1
  (151 shorter events, 55.7 us)
Async XLA Ops:
  28.5 60.4 %copy-start.13 = (f32[2,1024]{1,0:T(2,128)S(1)}, f32[2,1024]{1,0:T(2,128)}, u32[]{:S(2)}) copy-start(f32[2,1024]{1,0:T(2,128)} %param.20) | copy-start | bytes 24580
  28.5 60.4 %copy-start.14 = (f32[2,1024]{1,0:T(2,128)S(1)}, f32[2,1024]{1,0:T(2,128)}, u32[]{:S(2)}) copy-start(f32[2,1024]{1,0:T(2,128)} %param.19) | copy-start | bytes 24580
  28.5 61.0 %copy-start.15 = (f32[2,1024]{1,0:T(2,128)S(1)}, f32[2,1024]{1,0:T(2,128)}, u32[]{:S(2)}) copy-start(f32[2,1024]{1,0:T(2,128)} %param.18) | copy-start | bytes 24580
  28.5 61.0 %copy-start.16 = (f32[2,1024]{1,0:T(2,128)S(1)}, f32[2,1024]{1,0:T(2,128)}, u32[]{:S(2)}) copy-start(f32[2,1024]{1,0:T(2,128)} %param.17) | copy-start | bytes 24580
  28.5 61.6 %copy-start.19 = (f32[2,768]{1,0:T(2,128)S(1)}, f32[2,768]{1,0:T(2,128)}, u32[]{:S(2)}) copy-start(f32[2,768]{1,0:T(2,128)} %param.22) | copy-start | bytes 18436
  91.1 33.3 %copy-start.12 = (f32[2,1024]{1,0:T(2,128)S(1)}, f32[2,1024]{1,0:T(2,128)}, u32[]{:S(2)}) copy-start(f32[2,1024]{1,0:T(2,128)} %param.26) | copy-start | bytes 24580
  130.0 23.0 %copy-start.10 = (f32[2,1024]{1,0:T(2,128)S(1)}, f32[2,1024]{1,0:T(2,128)}, u32[]{:S(2)}) copy-start(f32[2,1024]{1,0:T(2,128)} %param.28) | copy-start | bytes 24580
  130.0 23.1 %copy-start.11 = (f32[2,1024]{1,0:T(2,128)S(1)}, f32[2,1024]{1,0:T(2,128)}, u32[]{:S(2)}) copy-start(f32[2,1024]{1,0:T(2,128)} %param.24) | copy-start | bytes 24580
  130.0 23.1 %copy-start = (f32[2,1,128,1024]{3,2,1,0:T(8,128)S(1)}, f32[2,1,128,1024]{3,2,1,0:T(8,128)}, u32[]{:S(2)}) copy-start(f32[2,1,128,1024]{3,2,1,0:T(8,128)} %param.15) | copy-start | bytes 3145732
  317.4 1.0 copy-start.4
  319.2 8.0 %copy-start.2 = (f32[256,1024]{1,0:T(8,128)S(1)}, f32[256,1024]{1,0:T(8,128)}, u32[]{:S(2)}) copy-start(f32[256,1024]{1,0:T(8,128)} %add_add_fusion.x) | copy-start | bytes 3145732
  375.1 124.3 %copy-start.21 = (f32[1,768]{1,0:T(1,128)S(1)}, f32[1,768]{1,0:T(1,128)}, u32[]{:S(2)}) copy-start(f32[1,768]{1,0:T(1,128)} %get-tuple-element.110) | copy-start | bytes 9220
  375.1 124.3 %copy-start.9 = (f32[4,1024]{1,0:T(4,128)S(1)}, f32[4,1024]{1,0:T(4,128)}, u32[]{:S(2)}) copy-start(f32[4,1024]{1,0:T(4,128)} %get-tuple-element.101) | copy-start | bytes 49156
  375.1 124.4 %copy-start.20 = (f32[1,768]{1,0:T(1,128)S(1)}, f32[1,768]{1,0:T(1,128)}, u32[]{:S(2)}) copy-start(f32[1,768]{1,0:T(1,128)} %get-tuple-element.111) | copy-start | bytes 9220
  375.1 124.4 %copy-start.8 = (f32[4,1024]{1,0:T(4,128)S(1)}, f32[4,1024]{1,0:T(4,128)}, u32[]{:S(2)}) copy-start(f32[4,1024]{1,0:T(4,128)} %get-tuple-element.103) | copy-start | bytes 49156
  496.0 137.0 %copy-start.18 = (f32[2,1024]{1,0:T(2,128)S(1)}, f32[2,1024]{1,0:T(2,128)}, u32[]{:S(2)}) copy-start(f32[2,1024]{1,0:T(2,128)} %get-tuple-element.100) | copy-start | bytes 24580
  496.0 137.0 %copy-start.17 = (f32[2,1024]{1,0:T(2,128)S(1)}, f32[2,1024]{1,0:T(2,128)}, u32[]{:S(2)}) copy-start(f32[2,1024]{1,0:T(2,128)} %get-tuple-element.102) | copy-start | bytes 24580
  629.7 128.2 %copy-start.7 = (f32[2,1024]{1,0:T(2,128)}, f32[2,1024]{1,0:T(2,128)S(1)}, u32[]{:S(2)}) copy-start(f32[2,1024]{1,0:T(2,128)S(1)} %get-tuple-element.246) | copy-start | bytes 24580
  721.1 4.9 copy-start.6
  727.8 26.3 %copy-start.1 = (f32[2,1,128,1024]{3,2,1,0:T(8,128)S(1)}, f32[2,1,128,1024]{3,2,1,0:T(8,128)}, u32[]{:S(2)}) copy-start(f32[2,1,128,1024]{3,2,1,0:T(8,128)} %param.15) | copy-start | bytes 3145732
  727.8 26.3 %copy-start.3 = (f32[2,1,128,1024]{3,2,1,0:T(8,128)S(1)}, f32[2,1,128,1024]{3,2,1,0:T(8,128)}, u32[]{:S(2)}) copy-start(f32[2,1,128,1024]{3,2,1,0:T(8,128)} %param.29) | copy-start | bytes 3145732
  727.8 26.3 %copy-start.5 = (f32[2,1,128,1024]{3,2,0,1:T(8,128)S(1)}, f32[2,1,128,1024]{3,2,0,1:T(8,128)}, u32[]{:S(2)}) copy-start(f32[2,1,128,1024]{3,2,0,1:T(8,128)} %copy-done.4) | copy-start | bytes 3145732

commit v2 on v1

--- a/solution.py
+++ b/solution.py
@@ -60,53 +60,147 @@
     )
 
 
-def gather_kernel(src, out, ssem, rsem, fs, fr, lsem):
-    b = lax.axis_index("batch")
-    s, c, k = places()
-    p = b * 8 + c
-    partner = {"seq": s + 1 - 2 * k}
-    others = []
-    for d in range(1, 16):
-        p2 = lax.rem(p + d, 16)
-        others.append({"batch": p2 // 8, "seq": lax.rem(p2, 8) * 2 + k})
-    greet(others + [partner])
-    mine = b * 16 + s
-    local = pltpu.make_async_copy(src, out.at[mine], lsem)
-    local.start()
-    copies = [
-        remote(src, out.at[mine], ssem.at[d], rsem.at[d], peer) for d, peer in enumerate(others)
-    ]
-    for copy in copies:
+class Spot:
+    def __init__(self):
+        b = lax.axis_index("batch")
+        s, c, self.core = places()
+        self.pos = (lax.rem(c, 4), (c // 4) * 2 + b)
+        self.partner = {"seq": s + 1 - 2 * self.core}
+
+    def ring(self, r):
+        k = self.core
+        return [r, lax.rem(r + 3 - 2 * k, 4), lax.rem(r + 1 + 2 * k, 4), lax.rem(r + 2, 4)]
+
+    def device(self, x, y):
+        return {"batch": lax.rem(y, 2), "seq": ((y // 2) * 4 + x) * 2 + self.core}
+
+    def neighbours(self):
+        x, y = self.pos
+        xs, ys = self.ring(x), self.ring(y)
+        return [self.device(x2, y) for x2 in xs[1:3]] + [self.device(x, y2) for y2 in ys[1:3]]
+
+
+def flat(x, y):
+    return lax.rem(y, 2) * 8 + (y // 2) * 4 + x
+
+
+def drive(jobs):
+    jobs = list(jobs)
+    while jobs:
+        for job in list(jobs):
+            try:
+                next(job)
+            except StopIteration:
+                jobs.remove(job)
+
+
+def ring_gather(spot, src, out, first, ss, rs, fs, fr, ls):
+    k = spot.core
+    along, other = spot.ring(spot.pos[first]), spot.ring(spot.pos[1 - first])
+
+    def place(i, j):
+        at = (along[i], other[j])
+        return at if first == 0 else at[::-1]
+
+    def slot(i, j):
+        return out.at[flat(*place(i, j)), k]
+
+    sent, passed = [], []
+
+    def send(i, j, idx, to):
+        piece = slot(i, j)
+        copy = remote(src if (i, j) == (0, 0) else piece, piece, ss.at[idx], rs.at[idx], to)
         copy.start()
-    onward = [remote(src, out.at[mine], fs.at[0], fr.at[0], partner)]
-    onward[0].start()
-    for d in range(1, 16):
-        copies[d - 1].wait_recv()
-        p2 = lax.rem(p - d + 16, 16)
-        at = out.at[(p2 // 8) * 16 + lax.rem(p2, 8) * 2 + k]
-        copy = remote(at, at, fs.at[d], fr.at[d], partner)
+        sent.append(copy)
+        return copy
+
+    def share(i, j):
+        piece, idx = slot(i, j), 4 * i + j
+        copy = remote(
+            src if idx == 0 else piece, piece, fs.at[idx], fr.at[idx], spot.partner
+        )
         copy.start()
-        onward.append(copy)
-    local.wait()
-    for copy in copies:
+        passed.append(copy)
+
+    ahead1, behind1 = spot.device(*place(2, 0)), spot.device(*place(1, 0))
+    ahead2, behind2 = spot.device(*place(0, 2)), spot.device(*place(0, 1))
+    own = pltpu.make_async_copy(src, slot(0, 0), ls)
+    own.start()
+    m0 = send(0, 0, 0, ahead1)
+    m1 = send(0, 0, 1, behind1)
+
+    def second(i):
+        return send(i, 0, 3 + 3 * i, ahead2), send(i, 0, 4 + 3 * i, behind2)
+
+    n = {0: second(0)}
+    share(0, 0)
+    yield
+    m0.wait_recv()
+    m2 = send(1, 0, 2, ahead1)
+    n[1] = second(1)
+    share(1, 0)
+    yield
+    m1.wait_recv()
+    n[2] = second(2)
+    share(2, 0)
+    yield
+    far = {}
+
+    def middle(i):
+        n[i][0].wait_recv()
+        far[i] = send(i, 1, 5 + 3 * i, ahead2)
+        share(i, 1)
+        n[i][1].wait_recv()
+        share(i, 2)
+
+    middle(0)
+    yield
+    m2.wait_recv()
+    n[3] = second(3)
+    share(3, 0)
+    yield
+    for i in range(1, 4):
+        middle(i)
+        yield
+    for i in range(4):
+        far[i].wait_recv()
+        share(i, 3)
+        yield
+    own.wait()
+    for copy in sent:
         copy.wait_send()
-    for copy in onward:
+    for copy in passed:
         copy.wait()
 
 
-def gather_weights(shard):
-    rows, cols = shard.shape
+def gather_sems():
     dma = pltpu.SemaphoreType.DMA
+    return [dma((15,)), dma((15,)), dma((16,)), dma((16,)), dma(())]
+
+
+def gather_kernel(firsts, *refs):
+    count = len(firsts)
+    srcs, outs, sems = refs[:count], refs[count : 2 * count], refs[2 * count :]
+    spot = Spot()
+    greet(spot.neighbours() + [spot.partner])
+    drive(
+        ring_gather(spot, srcs[a], outs[a], firsts[a], *sems[5 * a : 5 * a + 5])
+        for a in range(count)
+    )
+
+
+def gather_plane(arrays, firsts, ident):
+    count = len(arrays)
     return comm_call(
-        gather_kernel,
-        jax.ShapeDtypeStruct((32, rows, cols), shard.dtype),
-        [dma((15,)), dma((15,)), dma((16,)), dma((16,)), dma(())],
-        1,
+        functools.partial(gather_kernel, firsts),
+        tuple(jax.ShapeDtypeStruct((16, 2, *a.shape), a.dtype) for a in arrays),
+        [sem for _ in arrays for sem in gather_sems()],
+        ident,
         pl.ANY,
         pl.ANY,
-        1,
-        "gather_weights",
-    )(shard).reshape(32 * rows, cols)
+        count,
+        "gather_plane",
+    )(*arrays)
 
 
 def heads_out_kernel(src, kv_out, q_out, ssem, rsem, fs, fr, lsem):
@@ -249,107 +343,209 @@
     )(dq, dkv)
 
 
-def tensor_sum_kernel(part, out, got, ssem, rsem):
+def ring_sum(spot, part, out, rows, buf, held, ss, rs):
+    t, behind, ahead, across = spot.ring(lax.axis_index("tensor"))
+    to_ahead, to_behind = {"tensor": ahead}, {"tensor": behind}
+    sent = []
+
+    def send(src, dst, idx, to):
+        copy = remote(src, dst, ss.at[idx], rs.at[idx], to)
+        copy.start()
+        sent.append(copy)
+        return copy
+
+    far = send(part.at[across, rows], buf.at[0, rows], 0, to_ahead)
+    back = send(part.at[behind, rows], buf.at[2, rows], 2, to_behind)
+    yield
+    far.wait_recv()
+    held[rows] = (part[ahead, rows].astype(F32) + buf[0, rows].astype(F32)).astype(BF16)
+    on = send(held.at[rows], buf.at[1, rows], 1, to_ahead)
+    yield
+    back.wait_recv()
+    on.wait_recv()
+    total = part[t, rows].astype(F32) + buf[1, rows].astype(F32) + buf[2, rows].astype(F32)
+    out[t, rows] = total.astype(BF16)
+    mine, theirs = out.at[t, rows], out.at[behind, rows]
+    first = send(mine, mine, 3, to_ahead)
+    second = send(mine, mine, 4, to_behind)
+    yield
+    first.wait_recv()
+    third = send(theirs, theirs, 5, to_ahead)
+    yield
+    second.wait_recv()
+    third.wait_recv()
+    for copy in sent:
+        copy.wait_send()
+
+
+def direct_sum(vec, vec_out, got, ss, rs):
     t = lax.axis_index("tensor")
-    peers = [{"tensor": lax.rem(t + d, 4)} for d in range(1, 4)]
-    greet(peers)
     copies = []
-    for d, peer in enumerate(peers):
-        copies.append(
-            remote(part.at[lax.rem(t + d + 1, 4)], got.at[d], ssem.at[0, d], rsem.at[0, d], peer)
-        )
+    for d in range(3):
+        to = {"tensor": lax.rem(t + d + 1, 4)}
+        copies.append(remote(vec, got.at[t], ss.at[d], rs.at[d], to))
         copies[-1].start()
+    got[t] = vec[...]
+    yield
+    yield
+    yield
     for copy in copies:
-        copy.wait_recv()
-    total = part[t].astype(F32) + got[0].astype(F32) + got[1].astype(F32) + got[2].astype(F32)
-    out[t] = total.astype(BF16)
-    for d, peer in enumerate(peers):
-        copies.append(remote(out.at[t], out.at[t], ssem.at[1, d], rsem.at[1, d], peer))
-        copies[-1].start()
-    for copy in copies[:3]:
-        copy.wait_send()
-    for copy in copies[3:]:
         copy.wait()
-
-
-def tensor_sum(part):
+    vec_out[...] = (got[0] + got[1]) + (got[2] + got[3])
+
+
+def tensor_sum_kernel(count, *refs):
+    (part, *vec), (out, *vec_out) = refs[: 1 + count], refs[1 + count : 2 + 2 * count]
+    buf, held, s0, r0, s1, r1, *rest = refs[2 + 2 * count :]
+    spot = Spot()
+    t = lax.axis_index("tensor")
+    greet([{"tensor": lax.rem(t + d, 4)} for d in range(1, 4)])
+    jobs = [
+        ring_sum(spot, part, out, pl.ds(0, 128), buf, held, s0, r0),
+        ring_sum(spot, part, out, pl.ds(128, 128), buf, held, s1, r1),
+    ]
+    if count:
+        jobs.append(direct_sum(vec[0], vec_out[0], *rest))
+    drive(jobs)
+
+
+def tensor_sum(part, vec=None):
     dma = pltpu.SemaphoreType.DMA
+    count = 0 if vec is None else 1
+    shape = jax.ShapeDtypeStruct(part.shape, BF16)
+    scratch = [
+        pltpu.VMEM((3, *part.shape[1:]), BF16),
+        pltpu.VMEM(part.shape[1:], BF16),
+    ] + [dma((6,))] * 4
+    if vec is not None:
+        scratch += [pltpu.VMEM((4, *vec.shape), F32), dma((3,)), dma((3,))]
     return comm_call(
-        tensor_sum_kernel,
-        jax.ShapeDtypeStruct(part.shape, BF16),
-        [pltpu.VMEM((3, *part.shape[1:]), BF16), dma((2, 3)), dma((2, 3))],
-        5,
+        functools.partial(tensor_sum_kernel, count),
+        (shape,) if vec is None else (shape, jax.ShapeDtypeStruct(vec.shape, F32)),
+        scratch,
+        5 + 2 * count,
         pltpu.VMEM,
         pltpu.VMEM,
-        1,
+        1 + count,
         "tensor_sum",
-    )(part)
+    )(*((part,) if vec is None else (part, vec)))
+
+
+def ring_scatter(spot, src, out, first, pair, left, got, ps, pr, ss, rs):
+    k = spot.core
+    along, other = spot.ring(spot.pos[first]), spot.ring(spot.pos[1 - first])
+    kind = pair.dtype
+
+    def place(i, j):
+        at = (along[i], other[j])
+        return at if first == 0 else at[::-1]
+
+    order = (3, 2, 1, 0)
+    theirs = (0, 2, 1, 3)
+    pairs, sent = {}, []
+    for i in order:
+        for j in order:
+            at = flat(*place(theirs[i], theirs[j]))
+            idx = 4 * i + j
+            copy = remote(src.at[at, 1 - k], pair.at[idx], ps.at[idx], pr.at[idx], spot.partner)
+            copy.start()
+            pairs[idx] = copy
+    yield
+
+    def both(i, j):
+        pairs[4 * i + j].wait_recv()
+        return src[flat(*place(i, j)), k].astype(F32) + pair[4 * i + j].astype(F32)
+
+    def send(value, idx, to):
+        left[idx] = value.astype(kind)
+        copy = remote(left.at[idx], got.at[idx], ss.at[idx], rs.at[idx], to)
+        copy.start()
+        sent.append(copy)
+        return copy
+
+    ahead1, behind1 = spot.device(*place(2, 0)), spot.device(*place(1, 0))
+    ahead2, behind2 = spot.device(*place(0, 2)), spot.device(*place(0, 1))
+    far, on, back = {}, {}, {}
+    for j in order:
+        far[j] = send(both(3, j), j, ahead1)
+        back[j] = send(both(1, j), 8 + j, behind1)
+        yield
+    for j in order:
+        far[j].wait_recv()
+        on[j] = send(both(2, j) + got[j].astype(F32), 4 + j, ahead1)
+        yield
+
+    def settled(j):
+        on[j].wait_recv()
+        back[j].wait_recv()
+        return both(0, j) + got[4 + j].astype(F32) + got[8 + j].astype(F32)
+
+    far2 = send(settled(3), 12, ahead2)
+    yield
+    ready = settled(2)
+    back2 = send(settled(1), 14, behind2)
+    yield
+    far2.wait_recv()
+    on2 = send(ready + got[12].astype(F32), 13, ahead2)
+    total = settled(0)
+    yield
+    back2.wait_recv()
+    total = total + got[14].astype(F32)
+    on2.wait_recv()
+    out[...] = total + got[13].astype(F32)
+    for copy in pairs.values():
+        copy.wait_send()
+    for copy in sent:
+        copy.wait_send()
+
+
+def small_total(scatter, gather):
+    yield from scatter
+    yield from gather()
 
 
 def scatter_kernel(count, *refs):
-    ins, outs = refs[:count], refs[count : 2 * count]
-    rest = refs[2 * count :]
-    pair, sums, got = rest[:count], rest[count : 2 * count], rest[2 * count : 3 * count]
-    ps, pr, ssem, rsem = rest[3 * count :]
-    b = lax.axis_index("batch")
-    s, c, k = places()
-    p = b * 8 + c
-    partner = {"seq": s + 1 - 2 * k}
-    others = []
-    for d in range(1, 16):
-        p2 = lax.rem(p + d, 16)
-        others.append({"batch": p2 // 8, "seq": lax.rem(p2, 8) * 2 + k})
-    greet(others + [partner])
-    first = []
-    for d in range(16):
-        p2 = lax.rem(p + d + 1, 16)
-        for a in range(count):
-            copy = remote(
-                ins[a].at[p2, 1 - k], pair[a].at[p2], ps.at[a, d], pr.at[a, d], partner
-            )
-            copy.start()
-            first.append(copy)
-    second = []
-    for d in range(16):
-        p2 = lax.rem(p + d + 1, 16)
-        for a in range(count):
-            first[d * count + a].wait_recv()
-            total = ins[a][p2, k].astype(F32) + pair[a][p2].astype(F32)
-            if d < 15:
-                sums[a][d] = total.astype(BF16)
-                copy = remote(sums[a].at[d], got[a].at[d], ssem.at[a, d], rsem.at[a, d], others[d])
-                copy.start()
-                second.append(copy)
-            else:
-                outs[a][...] = total
-    for d in range(15):
-        for a in range(count):
-            second[d * count + a].wait_recv()
-            outs[a][...] += got[a][d].astype(F32)
-    for copy in first:
-        copy.wait_send()
-    for copy in second:
-        copy.wait_send()
-
-
-def scatter_sum(arrays):
-    count = len(arrays)
+    ins, outs = refs[: count + 1], refs[count + 1 : 2 * count + 2]
+    rest = refs[2 * count + 2 :]
+    spot = Spot()
+    greet(spot.neighbours() + [spot.partner])
+    args = [rest[7 * a : 7 * a + 7] for a in range(count + 1)]
+    jobs = [
+        ring_scatter(spot, ins[a], outs[a], (a + 1) % 2, *args[a]) for a in range(count)
+    ]
+    piece, *sems = rest[7 * count + 7 :]
+    small = ring_scatter(spot, ins[count], piece, 0, *args[count])
+    jobs.append(
+        small_total(small, lambda: ring_gather(spot, piece, outs[count], 0, *sems))
+    )
+    drive(jobs)
+
+
+def scatter_sum(arrays, small):
     dma = pltpu.SemaphoreType.DMA
-    shaped = [a.reshape(16, 2, 32, a.shape[1]) for a in arrays]
-    widths = [a.shape[1] for a in arrays]
+    ins = [a.reshape(16, 2, 32, a.shape[1]) for a in arrays] + [small]
+    scratch = []
+    for a in ins:
+        scratch += [
+            pltpu.VMEM((16, *a.shape[2:]), a.dtype),
+            pltpu.VMEM((15, *a.shape[2:]), a.dtype),
+            pltpu.VMEM((15, *a.shape[2:]), a.dtype),
+            dma((16,)),
+            dma((16,)),
+            dma((15,)),
+            dma((15,)),
+        ]
     return comm_call(
-        functools.partial(scatter_kernel, count),
-        tuple(jax.ShapeDtypeStruct((32, w), F32) for w in widths),
-        [pltpu.VMEM((16, 32, w), BF16) for w in widths]
-        + [pltpu.VMEM((15, 32, w), BF16) for w in widths]
-        + [pltpu.VMEM((15, 32, w), BF16) for w in widths]
-        + [dma((count, 16)), dma((count, 16)), dma((count, 15)), dma((count, 15))],
+        functools.partial(scatter_kernel, len(arrays)),
+        tuple(jax.ShapeDtypeStruct(a.shape[2:], F32) for a in ins[:-1])
+        + (jax.ShapeDtypeStruct(small.shape, F32),),
+        scratch + [pltpu.VMEM(small.shape[2:], F32)] + gather_sems(),
         6,
         pltpu.VMEM,
         pltpu.VMEM,
-        count,
+        len(ins),
         "scatter_sum",
-    )(*shaped)
+    )(*ins)
 
 
 def turned(values, cosine, sine):
@@ -366,7 +562,32 @@
     return centred * rstd, rstd
 
 
-def project_kernel(x, g1, b1, g2, b2, bias, weight, cosine, sine, h1, h2, qkv):
+def with_branch(x, branch, shift, out):
+    for t in range(4):
+        at = slice(256 * t, 256 * (t + 1))
+        out[:, at] = x[:, at] + branch[t].astype(F32) + shift[:, at]
+
+
+def norm_back(grad, z, x, out):
+    hat, rstd = normal(x[...])
+    flow = jnp.concatenate([z[t].astype(F32) for t in range(4)], axis=1)
+    out[...] = grad[...] + rstd * (
+        flow
+        - jnp.mean(flow, axis=-1, keepdims=True)
+        - hat * jnp.mean(flow * hat, axis=-1, keepdims=True)
+    )
+
+
+def project_kernel(*refs):
+    if len(refs) == 15:
+        x, branch, shift, *rest, x_out = refs
+        with_branch(x, branch, shift, x_out)
+        project_rows(x_out, *rest)
+    else:
+        project_rows(*refs)
+
+
+def project_rows(x, g1, b1, g2, b2, bias, weight, cosine, sine, h1, h2, qkv):
     hat, _ = normal(x[...])
     h1[...] = (hat * g1[...] + b1[...]).astype(BF16)
     h2[...] = (hat * g2[...] + b2[...]).astype(BF16)
@@ -410,18 +631,38 @@
     return [whole(a.shape) for a in arrays]
 
 
-def project(x, g1, b1, g2, b2, bias, gathered, cosine, sine):
+def project(x, g1, b1, g2, b2, bias, gathered, cosine, sine, branch=None, shift=None):
     sds = jax.ShapeDtypeStruct
+    more = () if branch is None else (branch, shift)
     return local_call(
         project_kernel,
         (
             sds((256, 1024), BF16),
             sds((256, 1024), BF16),
             sds((8, 2, 128, 128), BF16),
-        ),
-        wholes(x, g1, b1, g2, b2, bias) + [columns(768, 0)] + wholes(cosine, sine),
+        )
+        + ((sds((256, 1024), F32),) if more else ()),
+        wholes(x, *more, g1, b1, g2, b2, bias) + [columns(768, 0)] + wholes(cosine, sine),
         "project",
-    )(x, g1, b1, g2, b2, bias, gathered, cosine, sine)
+    )(x, *more, g1, b1, g2, b2, bias, gathered, cosine, sine)
+
+
+def add_branch(x, branch, shift):
+    return local_call(
+        with_branch,
+        jax.ShapeDtypeStruct(x.shape, F32),
+        wholes(x, branch, shift),
+        "add_branch",
+    )(x, branch, shift)
+
+
+def add_norm_back(grad, z, x):
+    return local_call(
+        norm_back,
+        jax.ShapeDtypeStruct(grad.shape, F32),
+        wholes(grad, z, x),
+        "add_norm_back",
+    )(grad, z, x)
 
 
 def scores_of(q, keys, low, high):
@@ -521,7 +762,16 @@
     )(ctx_in, h2, gathered, gathered, gathered, bias)
 
 
-def feed_back_kernel(
+def feed_back_kernel(*refs):
+    if len(refs) == 17:
+        before, z, x_before, *rest, grad = refs
+        norm_back(before, z, x_before, grad)
+        feed_back_rows(grad, *rest)
+    else:
+        feed_back_rows(*refs)
+
+
+def feed_back_rows(
     grad, x, g2, u, act, ctx, h2, dense, expand, shrink, dctx, wgrad, z2, small
 ):
     gb = grad[...].astype(BF16)
@@ -539,9 +789,9 @@
             if h % 2 == 0:
                 piece = pltpu.roll(piece, 64, axis=1)
             dctx[m * 4 + h] = jnp.where(lane >= 64, piece, 0.0).astype(BF16)
-    wgrad[:, 0:256] = dot(gb, ctx[...], 0, 0).astype(BF16)
-    wgrad[:, 256:1280] = dot(h2[...], du, 0, 0).astype(BF16)
-    wgrad[:, 1280:2304] = dot(gb, act[...], 0, 0).astype(BF16)
+    wgrad[:, 768:1024] = dot(gb, ctx[...], 0, 0).astype(BF16)
+    wgrad[:, 1024:2048] = dot(h2[...], du, 0, 0).astype(BF16)
+    wgrad[:, 2048:3072] = dot(gb, act[...], 0, 0).astype(BF16)
     dh2 = dot(du, expand[...], 1, 1)
     hat, _ = normal(x[...])
     z2[...] = dh2 * g2[...]
@@ -551,24 +801,26 @@
     small[3:4] = jnp.sum(du.astype(F32), axis=0, keepdims=True)
 
 
-def feed_back(grad, x, g2, u, act, ctx, h2, gathered):
+def feed_back(grad, x, g2, u, act, ctx, h2, gathered, z=None, x_before=None):
     sds = jax.ShapeDtypeStruct
+    more = () if z is None else (z, x_before)
     return local_call(
         feed_back_kernel,
         (
             sds((8, 128, 128), BF16),
-            sds((1024, 2304), BF16),
+            sds((1024, 3072), BF16),
             sds((256, 1024), F32),
             sds((4, 1024), F32),
-        ),
-        wholes(grad, x, g2, u, act, ctx, h2)
+        )
+        + ((sds((256, 1024), F32),) if more else ()),
+        wholes(grad, *more, x, g2, u, act, ctx, h2)
         + [columns(256, 3), columns(1024, 1), columns(1024, 2)],
         "feed_back",
-    )(grad, x, g2, u, act, ctx, h2, gathered, gathered, gathered)
+    )(grad, *more, x, g2, u, act, ctx, h2, gathered, gathered, gathered)
 
 
 def project_back_kernel(
-    dq, dkv, cosine, sine, h1, weight, z2, x, g1, wgrad, part, small, bias_grad, dproj
+    dq, dkv, cosine, sine, h1, weight, z2, x, g1, _, wgrad, part, small, bias_grad, dproj, narrow, sem
 ):
     cos, sin = cosine[...], -sine[...]
     lane = lax.broadcasted_iota(jnp.int32, (128, 128), 1)
@@ -585,29 +837,48 @@
                 lane < 64, left, pltpu.roll(right, 64, axis=1)
             ).astype(BF16)
     dp = dproj[...]
-    wgrad[...] = dot(h1[...], dp, 0, 0).astype(BF16)
+    narrow[...] = dot(h1[...], dp, 0, 0).astype(BF16)
+    copy = pltpu.make_async_copy(narrow, wgrad.at[:, 0:768], sem)
+    copy.start()
     bias_grad[...] = jnp.sum(dp.astype(F32), axis=0, keepdims=True)
     dh1 = dot(dp, weight[...], 1, 1)
     hat, _ = normal(x[...])
     small[0:1] = jnp.sum(dh1 * hat, axis=0, keepdims=True)
     small[1:2] = jnp.sum(dh1, axis=0, keepdims=True)
     in_quarters(dh1 * g1[...] + z2[...], part)
-
-
-def project_back(dq, dkv, cosine, sine, h1, gathered, z2, x, g1):
+    copy.wait()
+
+
+def project_back(dq, dkv, cosine, sine, h1, gathered, z2, x, g1, wgrad):
     sds = jax.ShapeDtypeStruct
-    return local_call(
+    return pl.pallas_call(
         project_back_kernel,
-        (
-            sds((1024, 768), BF16),
+        out_shape=(
+            sds((1024, 3072), BF16),
             sds((4, 256, 256), BF16),
             sds((2, 1024), F32),
             sds((1, 768), F32),
         ),
-        wholes(dq, dkv, cosine, sine, h1) + [columns(768, 0)] + wholes(z2, x, g1),
-        "project_back",
-        [pltpu.VMEM((256, 768), BF16)],
-    )(dq, dkv, cosine, sine, h1, gathered, z2, x, g1)
+        grid=(1,),
+        in_specs=wholes(dq, dkv, cosine, sine, h1)
+        + [columns(768, 0)]
+        + wholes(z2, x, g1)
+        + [pl.BlockSpec(memory_space=pl.ANY)],
+        out_specs=(
+            pl.BlockSpec(memory_space=pl.ANY),
+            whole((4, 256, 256)),
+            whole((2, 1024)),
+            whole((1, 768)),
+        ),
+        scratch_shapes=[
+            pltpu.VMEM((256, 768), BF16),
+            pltpu.VMEM((1024, 768), BF16),
+            pltpu.SemaphoreType.DMA(()),
+        ],
+        input_output_aliases={9: 0},
+        compiler_params=pltpu.CompilerParams(vmem_limit_bytes=VLIM),
+        name="project_back",
+    )(dq, dkv, cosine, sine, h1, gathered, z2, x, g1, wgrad)
 
 
 def head_order(value):
@@ -657,15 +928,6 @@
     cosine = jnp.concatenate([cos, cos, ones], axis=1)
     sine = jnp.concatenate([-sin, sin, zeros], axis=1)
 
-    idents = lax.all_gather(document_ids, "seq", axis=2, tiled=True)
-    mine = lax.dynamic_index_in_dim(idents[:, 0], unit_micro, 0, keepdims=False)
-    count0 = jnp.sum((mine == 0).astype(jnp.int32))
-    count1 = jnp.sum((mine == 1).astype(jnp.int32))
-    start = jnp.where(mine == 0, 0, jnp.where(mine == 1, count0, count0 + count1))
-    high = jnp.arange(2048, dtype=jnp.int32).reshape(8, 2, 128)
-    high = lax.dynamic_index_in_dim(high, core, 1, keepdims=False)[..., None]
-    low = lax.dynamic_index_in_dim(start.reshape(8, 2, 128), core, 1, keepdims=False)[..., None]
-
     shards = jnp.concatenate(
         [
             head_order(attn_weight),
@@ -675,14 +937,27 @@
         ],
         axis=2,
     )
-    weights = [gather_weights(shards[layer]) for layer in range(LAYERS)]
+    idents = jnp.pad(document_ids[:, 0], ((0, 6), (0, 0)))
+    early, late, idents = gather_plane([shards[0], shards[1], idents], (0, 1, 0), 1)
+    weights = [early.reshape(1024, 3072), late.reshape(1024, 3072)]
+    idents = idents.reshape(2, 16, 8, 128)
+    idents = lax.dynamic_index_in_dim(idents, lax.axis_index("batch"), 0, keepdims=False)
+    mine = lax.dynamic_index_in_dim(idents, unit_micro, 1, keepdims=False).reshape(2048)
+    count0 = jnp.sum((mine == 0).astype(jnp.int32))
+    count1 = jnp.sum((mine == 1).astype(jnp.int32))
+    start = jnp.where(mine == 0, 0, jnp.where(mine == 1, count0, count0 + count1))
+    high = jnp.arange(2048, dtype=jnp.int32).reshape(8, 2, 128)
+    high = lax.dynamic_index_in_dim(high, core, 1, keepdims=False)[..., None]
+    low = lax.dynamic_index_in_dim(start.reshape(8, 2, 128), core, 1, keepdims=False)[..., None]
     bias_order = head_order(attn_bias)
 
     x = hidden_in.reshape(256, 1024)
+    shift = dense_bias + shrink_bias
     kept = []
+    branch = ()
     for layer in range(LAYERS):
         row = slice(layer, layer + 1)
-        h1, h2, qkv = project(
+        h1, h2, qkv, *fresh = project(
             x,
             first_gain[row],
             first_shift[row],
@@ -692,45 +967,46 @@
             weights[layer],
             cosine,
             sine,
+            *branch,
         )
+        x = fresh[0] if fresh else x
         kv, q = heads_out(qkv)
         ctx_out, lse = attend(kv, q, low, high)
         ctx_in = swap_chips(ctx_out)
         u, act, ctx, part = feed(ctx_in, h2, weights[layer], expand_bias[row])
         kept.append((x, h1, h2, kv, q, lse, u, act, ctx))
-        x = x + from_quarters(tensor_sum(part)) + dense_bias[row] + shrink_bias[row]
-    hidden_out = x.reshape(2, 1, 128, 1024)
+        branch = (tensor_sum(part)[0], shift[row])
+    hidden_out = add_branch(x, *branch).reshape(2, 1, 128, 1024)
 
     grad = output_grad.reshape(256, 1024)
-    wide, narrow, by_all, by_rows = [None] * 2, [None] * 2, [None] * 2, [None] * 2
+    wgrads, by_all, by_rows = [None] * 2, [None] * 2, [None] * 2
+    before = ()
     for layer in reversed(range(LAYERS)):
         row = slice(layer, layer + 1)
         x, h1, h2, kv, q, lse, u, act, ctx = kept[layer]
-        dctx, wide[layer], z2, small2 = feed_back(
-            grad, x, second_gain[row], u, act, ctx, h2, weights[layer]
+        dctx, wgrad, z2, small2, *fresh = feed_back(
+            grad, x, second_gain[row], u, act, ctx, h2, weights[layer], *before
         )
+        grad = fresh[0] if fresh else grad
         dctx_in = swap_chips(dctx)
         dq, dkv = attend_back(kv, q, dctx_in, lse, low, high)
         dq_in, dkv_in = heads_back(dq, dkv)
-        narrow[layer], part, small1, bias_grad = project_back(
-            dq_in, dkv_in, cosine, sine, h1, weights[layer], z2, x, first_gain[row]
+        wgrads[layer], part, small1, bias_grad = project_back(
+            dq_in, dkv_in, cosine, sine, h1, weights[layer], z2, x, first_gain[row], wgrad
         )
-        z = from_quarters(tensor_sum(part))
-        hat, rstd = normal(x)
-        grad = grad + rstd * (
-            z
-            - jnp.mean(z, axis=-1, keepdims=True)
-            - hat * jnp.mean(z * hat, axis=-1, keepdims=True)
-        )
-        by_all[layer] = jnp.concatenate([small1, small2[:2]], axis=0)
+        z, by_all[layer] = tensor_sum(part, jnp.concatenate([small1, small2[:2]], axis=0))
+        before = (z, x)
         by_rows[layer] = jnp.concatenate([bias_grad[0], small2[2], small2[3]], axis=0)
-    input_grad = grad.reshape(2, 1, 128, 1024)
-
-    sums = scatter_sum([narrow[0], narrow[1], wide[0], wide[1]])
-    narrow_sum = head_order_back(jnp.stack(sums[:2]))
-    wide_sum = jnp.stack(sums[2:])
-    norms = lax.psum(jnp.stack(by_all), ("batch", "seq", "tensor"))
-    rows = lax.psum(jnp.stack(by_rows), ("batch", "seq"))
+    input_grad = add_norm_back(grad, *before).reshape(2, 1, 128, 1024)
+
+    small = jnp.concatenate([v.reshape(-1) for v in by_all + by_rows]).reshape(32, 432)
+    small = jnp.pad(small, ((0, 0), (0, 592))).reshape(16, 2, 8, 128)
+    *sums, small = scatter_sum(wgrads, small)
+    total = jnp.stack(sums)
+    narrow_sum = head_order_back(total[..., :768])
+    wide_sum = total[..., 768:]
+    small = small.reshape(32, 1024)[:, :432].reshape(13824)
+    norms, rows = small[:8192].reshape(2, 4, 1024), small[8192:].reshape(2, 2816)
     branch_bias = rows[:, 768:1792]
     return (
         hidden_out,

time: 771 us -> 411 us (0.53)
  blocking collectives: 217 us -> 0 us
  Pallas kernels: 477 us -> 368 us
  other arithmetic: 25.5 us -> 10.3 us
  local copies, waits for them, and re-layouts: 36.8 us -> 23.7 us
    psum x2 -> x0, blocking collectives: 194 us -> none  [the longest x1 129 us: local(): rows = lax.psum(jnp.stack(by_rows), ('batch', 'seq'))]
    pallas_call x11 -> x12, Pallas kernels: 328 us -> 222 us  [the longest x4 80.3 us: tensor_sum(): comm_call(functools.partial(tensor_sum_kernel, count), (shape,) if vec is...]
    all_gather x1 -> x0, blocking collectives: 22.6 us -> none  [local(): idents = lax.all_gather(document_ids, 'seq', axis=2, tiled=True)]
    convert_element_type x12 -> x0, local copies, waits for them, and re-layouts: 19.1 us -> none  [from_quarters(): return value.transpose(1, 0, 2).reshape(256, 1024).astype(F32)]
where the time goes in v2:
time: 411 us; the launch traced here: 405 us
  Pallas kernels  368 us (90%)
  local copies, waits for them, and re-layouts  23.7 us (6%)
  other arithmetic  10.3 us (3%)
    pallas_call x4, Pallas kernels, tensor_sum(): comm_call(functools.partial(tensor_sum_kernel, count), (shape,) if vec is...  80.3 us
    pallas_call x1, Pallas kernels, scatter_sum(): comm_call(functools.partial(scatter_kernel, len(arrays)), tuple((jax.Shap...  65 us
    pallas_call x1, Pallas kernels, gather_plane(): comm_call(functools.partial(gather_kernel, firsts), tuple((jax.ShapeDtype...  39.9 us
    pallas_call x4, Pallas kernels, swap_chips(): comm_call(swap_kernel, jax.ShapeDtypeStruct(blocks.shape, blocks.dtype),...  37.9 us
    pallas_call x2, Pallas kernels, heads_back(): comm_call(heads_back_kernel, (shape, shape), [pltpu.VMEM((8, 128, 128), F...  27.9 us
    pallas_call x2, Pallas kernels, attend_back(): local_call(attend_back_kernel, (sds((8, 128, 128), BF16), sds((2, 8, 128,...  25.6 us
    pallas_call x2, Pallas kernels, heads_out(): comm_call(heads_out_kernel, (jax.ShapeDtypeStruct((16, 128, 128), BF16),...  23.1 us
    pallas_call x2, Pallas kernels, feed_back(): local_call(feed_back_kernel, (sds((8, 128, 128), BF16), sds((1024, 3072),...  19.5 us

profile of v2, /device:TPU:24, one launch (start us, length us, event | category | flops | bytes accessed | tf_op | source)
XLA Modules:
  0.0 405.0 jit_solution(3645048397330252764)
XLA Ops:
  7.3 39.9 %gather_plane.1 = (bf16[16,2,32,3072]{3,2,1,0:T(8,128)(2,1)}, bf16[16,2,32,3072]{3,2,1,0:T(8,128)(2,1)}, s32[16,2,8,128]{3,2,1,0:T(8,128)}) custom-call(bf16[32,3072]{1,0:T(8,128)(2,1)} %get-tuple-element.195.refs_0_, bf16[32,3072]{1,0:T(8,128)(2,1)} %get-tuple-element.194.refs_1_, s32[8,128]{1,0:T(8,128)} %pad.8.refs_2_), custom_call_target="tpu_custom_call" | custom-call | tf_op jit(solution)/shard_map/gather_plane/pallas_call | solution.py:194
  53.9 1.4 fusion.10
  55.3 1.4 fusion.12
  58.3 4.1 %project.2 = (bf16[256,1024]{1,0:T(8,128)(2,1)}, bf16[256,1024]{1,0:T(8,128)(2,1)}, bf16[8,2,128,128]{3,2,1,0:T(8,128)(2,1)}) custom-call(f32[256,1024]{1,0:T(8,128)} %bitcast.82, f32[1,1024]{1,0:T(1,128)} %get-tuple-element.229.refs_1_.g1, f32[1,1024]{1,0:T(1,128)} %get-tuple-element.215.refs_2_, f32[1,1024]{1,0:T(1,128)} %get-tuple-element.227.refs_3_.refs_4_, ...), custom_call_target="tpu_custom_call" | custom-call | tf_op jit(solution)/shard_map/project/pallas_call | solution.py:637
  62.4 12.5 %heads_out.2 = (bf16[16,128,128]{2,1,0:T(8,128)(2,1)}, bf16[8,128,128]{2,1,0:T(8,128)(2,1)}) custom-call(bf16[8,2,128,128]{3,2,1,0:T(8,128)(2,1)} %get-tuple-element.73.src), custom_call_target="tpu_custom_call" | custom-call | tf_op jit(solution)/shard_map/heads_out/pallas_call | solution.py:249
  74.9 6.7 %attend.2 = (bf16[8,128,128]{2,1,0:T(8,128)(2,1)}, f32[8,128,1]{2,1,0:T(8,128)}) custom-call(bf16[16,128,128]{2,1,0:T(8,128)(2,1)} %get-tuple-element.74.kv, bf16[8,128,128]{2,1,0:T(8,128)(2,1)} %get-tuple-element.75.q, s32[8,128,1]{2,1,0:T(8,128)} %copy.65.low, s32[8,128,1]{2,1,0:T(8,128)} %copy.66.high), custom_call_target="tpu_custom_call" | custom-call | tf_op jit(solution)/shard_map/attend/pallas_call | solution.py:689
  81.6 9.9 %swap_chips.4.ctx_in = bf16[8,128,128]{2,1,0:T(8,128)(2,1)} custom-call(bf16[8,128,128]{2,1,0:T(8,128)(2,1)} %get-tuple-element.77.src), custom_call_target="tpu_custom_call" | custom-call | tf_op jit(solution)/shard_map/swap_chips/pallas_call | solution.py:282
  92.2 5.0 %feed.2 = (f32[256,1024]{1,0:T(8,128)}, bf16[256,1024]{1,0:T(8,128)(2,1)}, bf16[256,256]{1,0:T(8,128)(2,1)}, bf16[4,256,256]{2,1,0:T(8,128)(2,1)}) custom-call(bf16[8,128,128]{2,1,0:T(8,128)(2,1)} %swap_chips.4.ctx_in, bf16[256,1024]{1,0:T(8,128)(2,1)} %get-tuple-element.78.h2.refs_8_, bf16[1024,3072]{1,0:T(8,128)(2,1)} %bitcast.67, ...), custom_call_target="tpu_custom_call" | custom-call | tf_op jit(solution)/shard_map/feed/pallas_call | solution.py:752
  97.2 21.8 %tensor_sum.4.refs_1_ = bf16[4,256,256]{2,1,0:T(8,128)(2,1)} custom-call(bf16[4,256,256]{2,1,0:T(8,128)(2,1)} %get-tuple-element.79.refs_0_), custom_call_target="tpu_custom_call" | custom-call | tf_op jit(solution)/shard_map/tensor_sum/pallas_call | solution.py:422
  119.6 4.5 %project.3 = (bf16[256,1024]{1,0:T(8,128)(2,1)}, bf16[256,1024]{1,0:T(8,128)(2,1)}, bf16[8,2,128,128]{3,2,1,0:T(8,128)(2,1)}, f32[256,1024]{1,0:T(8,128)}) custom-call(f32[256,1024]{1,0:T(8,128)} %bitcast.83, bf16[4,256,256]{2,1,0:T(8,128)(2,1)} %tensor_sum.4.refs_1_, f32[1,1024]{1,0:T(1,128)} %get-tuple-element.207.refs_2_, ...), custom_call_target="tpu_custom_call" | custom-call | tf_op jit(solution)/shard_map/project/pallas_call | solution.py:637
  124.1 10.6 %heads_out.3 = (bf16[16,128,128]{2,1,0:T(8,128)(2,1)}, bf16[8,128,128]{2,1,0:T(8,128)(2,1)}) custom-call(bf16[8,2,128,128]{3,2,1,0:T(8,128)(2,1)} %get-tuple-element.82.src), custom_call_target="tpu_custom_call" | custom-call | tf_op jit(solution)/shard_map/heads_out/pallas_call | solution.py:249
  134.7 6.7 %attend.3 = (bf16[8,128,128]{2,1,0:T(8,128)(2,1)}, f32[8,128,1]{2,1,0:T(8,128)}) custom-call(bf16[16,128,128]{2,1,0:T(8,128)(2,1)} %get-tuple-element.83.kv, bf16[8,128,128]{2,1,0:T(8,128)(2,1)} %get-tuple-element.84.q, s32[8,128,1]{2,1,0:T(8,128)} %copy.65.low, s32[8,128,1]{2,1,0:T(8,128)} %copy.66.high), custom_call_target="tpu_custom_call" | custom-call | tf_op jit(solution)/shard_map/attend/pallas_call | solution.py:689
  141.4 9.3 %swap_chips.5.ctx_in = bf16[8,128,128]{2,1,0:T(8,128)(2,1)} custom-call(bf16[8,128,128]{2,1,0:T(8,128)(2,1)} %get-tuple-element.85.src), custom_call_target="tpu_custom_call" | custom-call | tf_op jit(solution)/shard_map/swap_chips/pallas_call | solution.py:282
  150.8 5.0 %feed.3 = (f32[256,1024]{1,0:T(8,128)}, bf16[256,1024]{1,0:T(8,128)(2,1)}, bf16[256,256]{1,0:T(8,128)(2,1)}, bf16[4,256,256]{2,1,0:T(8,128)(2,1)}) custom-call(bf16[8,128,128]{2,1,0:T(8,128)(2,1)} %swap_chips.5.ctx_in, bf16[256,1024]{1,0:T(8,128)(2,1)} %get-tuple-element.86.h2.refs_6_, bf16[1024,3072]{1,0:T(8,128)(2,1)} %bitcast.75, ...), custom_call_target="tpu_custom_call" | custom-call | tf_op jit(solution)/shard_map/feed/pallas_call | solution.py:752
  155.8 9.0 %feed_back.2 = (bf16[8,128,128]{2,1,0:T(8,128)(2,1)}, bf16[1024,3072]{1,0:T(8,128)(2,1)}, f32[256,1024]{1,0:T(8,128)}, f32[4,1024]{1,0:T(4,128)}) custom-call(f32[256,1024]{1,0:T(8,128)} %bitcast.89, f32[256,1024]{1,0:T(8,128)} %get-tuple-element.81.x.refs_1_.refs_2_, f32[1,1024]{1,0:T(1,128)} %get-tuple-element.228.refs_5_.refs_2_, ...), custom_call_target="tpu_custom_call" | custom-call | tf_op jit(solution)/shard_map/feed_back/pallas_call | solution.py:807
  164.8 9.3 %swap_chips.6.dctx = bf16[8,128,128]{2,1,0:T(8,128)(2,1)} custom-call(bf16[8,128,128]{2,1,0:T(8,128)(2,1)} %get-tuple-element.91.src), custom_call_target="tpu_custom_call" | custom-call | tf_op jit(solution)/shard_map/swap_chips/pallas_call | solution.py:282
  174.1 17.7 %attend_back.2 = (bf16[8,128,128]{2,1,0:T(8,128)(2,1)}, f32[2,8,128,128]{3,2,1,0:T(8,128)}) custom-call(bf16[16,128,128]{2,1,0:T(8,128)(2,1)} %get-tuple-element.83.kv, bf16[8,128,128]{2,1,0:T(8,128)(2,1)} %get-tuple-element.84.q, bf16[8,128,128]{2,1,0:T(8,128)(2,1)} %swap_chips.6.dctx, f32[8,128,1]{2,1,0:T(8,128)} %get-tuple-element.92.lse, ...), custom_call_target="tpu_custom_call" | custom-call | tf_op jit(solution)/shard_map/attend_back/pallas_call | solution.py:721
  191.8 13.8 %heads_back.2 = (bf16[8,128,128]{2,1,0:T(8,128)(2,1)}, bf16[8,128,128]{2,1,0:T(8,128)(2,1)}) custom-call(bf16[8,128,128]{2,1,0:T(8,128)(2,1)} %get-tuple-element.93.dq, f32[2,8,128,128]{3,2,1,0:T(8,128)} %get-tuple-element.94.dkv), custom_call_target="tpu_custom_call" | custom-call | tf_op jit(solution)/shard_map/heads_back/pallas_call | solution.py:327
  205.7 5.6 %project_back.2 = (bf16[1024,3072]{1,0:T(8,128)(2,1)}, bf16[4,256,256]{2,1,0:T(8,128)(2,1)}, f32[2,1024]{1,0:T(2,128)}, f32[1,768]{1,0:T(1,128)}) custom-call(bf16[8,128,128]{2,1,0:T(8,128)(2,1)} %get-tuple-element.95.dq, bf16[8,128,128]{2,1,0:T(8,128)(2,1)} %get-tuple-element.96.dkv, ...), custom_call_target="tpu_custom_call", output_to_operand_aliasing={{0}: (9, {})} | custom-call | tf_op jit(solution)/shard_map/project_back/pallas_call | solution.py:854
  212.7 19.5 %tensor_sum.6 = (bf16[4,256,256]{2,1,0:T(8,128)(2,1)}, f32[4,1024]{1,0:T(4,128)}) custom-call(bf16[4,256,256]{2,1,0:T(8,128)(2,1)} %get-tuple-element.100.refs_0_, f32[4,1024]{1,0:T(4,128)} %pad_maximum_fusion.5.refs_1_), custom_call_target="tpu_custom_call" | custom-call | tf_op jit(solution)/shard_map/tensor_sum/pallas_call | solution.py:422
  232.2 10.5 %feed_back.3 = (bf16[8,128,128]{2,1,0:T(8,128)(2,1)}, bf16[1024,3072]{1,0:T(8,128)(2,1)}, f32[256,1024]{1,0:T(8,128)}, f32[4,1024]{1,0:T(4,128)}, f32[256,1024]{1,0:T(8,128)}) custom-call(f32[256,1024]{1,0:T(8,128)} %bitcast.90, bf16[4,256,256]{2,1,0:T(8,128)(2,1)} %get-tuple-element.103.refs_1_, f32[256,1024]{1,0:T(8,128)} %get-tuple-element.81.x.refs_1_.refs_2_, ...), custom_call_target="tpu_custom_call" | custom-call | tf_op jit(solution)/shard_map/feed_back/pallas_call | solution.py:807
  242.7 9.3 %swap_chips.7.dctx = bf16[8,128,128]{2,1,0:T(8,128)(2,1)} custom-call(bf16[8,128,128]{2,1,0:T(8,128)(2,1)} %get-tuple-element.108.src), custom_call_target="tpu_custom_call" | custom-call | tf_op jit(solution)/shard_map/swap_chips/pallas_call | solution.py:282
  252.0 7.9 %attend_back.3 = (bf16[8,128,128]{2,1,0:T(8,128)(2,1)}, f32[2,8,128,128]{3,2,1,0:T(8,128)}) custom-call(bf16[16,128,128]{2,1,0:T(8,128)(2,1)} %get-tuple-element.74.kv, bf16[8,128,128]{2,1,0:T(8,128)(2,1)} %get-tuple-element.75.q, bf16[8,128,128]{2,1,0:T(8,128)(2,1)} %swap_chips.7.dctx, f32[8,128,1]{2,1,0:T(8,128)} %get-tuple-element.109.lse, ...), custom_call_target="tpu_custom_call" | custom-call | tf_op jit(solution)/shard_map/attend_back/pallas_call | solution.py:721
  259.9 14.1 %heads_back.3 = (bf16[8,128,128]{2,1,0:T(8,128)(2,1)}, bf16[8,128,128]{2,1,0:T(8,128)(2,1)}) custom-call(bf16[8,128,128]{2,1,0:T(8,128)(2,1)} %get-tuple-element.110.dq, f32[2,8,128,128]{3,2,1,0:T(8,128)} %get-tuple-element.111.dkv), custom_call_target="tpu_custom_call" | custom-call | tf_op jit(solution)/shard_map/heads_back/pallas_call | solution.py:327
  274.0 5.6 %project_back.3 = (bf16[1024,3072]{1,0:T(8,128)(2,1)}, bf16[4,256,256]{2,1,0:T(8,128)(2,1)}, f32[2,1024]{1,0:T(2,128)}, f32[1,768]{1,0:T(1,128)}) custom-call(bf16[8,128,128]{2,1,0:T(8,128)(2,1)} %get-tuple-element.112.dq, bf16[8,128,128]{2,1,0:T(8,128)(2,1)} %get-tuple-element.113.dkv, ...), custom_call_target="tpu_custom_call", output_to_operand_aliasing={{0}: (9, {})} | custom-call | tf_op jit(solution)/shard_map/project_back/pallas_call | solution.py:854
  281.0 21.0 %tensor_sum.7 = (bf16[4,256,256]{2,1,0:T(8,128)(2,1)}, f32[4,1024]{1,0:T(4,128)}) custom-call(bf16[4,256,256]{2,1,0:T(8,128)(2,1)} %get-tuple-element.117.refs_0_, f32[4,1024]{1,0:T(4,128)} %pad_maximum_fusion.6.refs_1_), custom_call_target="tpu_custom_call" | custom-call | tf_op jit(solution)/shard_map/tensor_sum/pallas_call | solution.py:422
  304.4 65.0 %scatter_sum.1 = (f32[32,3072]{1,0:T(8,128)}, f32[32,3072]{1,0:T(8,128)}, f32[16,2,8,128]{3,2,1,0:T(8,128)}) custom-call(bf16[16,2,32,3072]{3,2,1,0:T(8,128)(2,1)} %bitcast.87, bf16[16,2,32,3072]{3,2,1,0:T(8,128)(2,1)} %bitcast.88, f32[16,2,8,128]{3,2,1,0:T(8,128)} %bitcast.99), custom_call_target="tpu_custom_call" | custom-call | tf_op jit(solution)/shard_map/scatter_sum/pallas_call | solution.py:538
  369.4 1.9 fusion
  373.3 1.4 maximum_bitcast_fusion
  380.4 3.3 add_norm_back.1
  383.7 18.0 %tensor_sum.5.branch = bf16[4,256,256]{2,1,0:T(8,128)(2,1)} custom-call(bf16[4,256,256]{2,1,0:T(8,128)(2,1)} %get-tuple-element.87.refs_0_), custom_call_target="tpu_custom_call" | custom-call | tf_op jit(solution)/shard_map/tensor_sum/pallas_call | solution.py:422
  401.7 2.5 add_branch.1
  (98 shorter events, 27.8 us)
Async XLA Ops:
  7.3 84.3 %copy-start.6 = (f32[2,1024]{1,0:T(2,128)S(1)}, f32[2,1024]{1,0:T(2,128)}, u32[]{:S(2)}) copy-start(f32[2,1024]{1,0:T(2,128)} %param.26) | copy-start | bytes 24580
  92.2 26.8 %copy-start.4 = (f32[2,1024]{1,0:T(2,128)S(1)}, f32[2,1024]{1,0:T(2,128)}, u32[]{:S(2)}) copy-start(f32[2,1024]{1,0:T(2,128)} %param.24) | copy-start | bytes 24580
  92.2 26.8 %copy-start.5 = (f32[2,1024]{1,0:T(2,128)S(1)}, f32[2,1024]{1,0:T(2,128)}, u32[]{:S(2)}) copy-start(f32[2,1024]{1,0:T(2,128)} %param.28) | copy-start | bytes 24580
  205.7 5.6 %copy-start.1 = (f32[4,1024]{1,0:T(4,128)S(1)}, f32[4,1024]{1,0:T(4,128)}, u32[]{:S(2)}) copy-start(f32[4,1024]{1,0:T(4,128)} %get-tuple-element.102) | copy-start | bytes 49156
  274.0 5.7 %copy-start.2 = (f32[4,1024]{1,0:T(4,128)S(1)}, f32[4,1024]{1,0:T(4,128)}, u32[]{:S(2)}) copy-start(f32[4,1024]{1,0:T(4,128)} %get-tuple-element.119) | copy-start | bytes 49156
  274.0 28.7 %copy-start.3 = (f32[4,1024]{1,0:T(4,128)S(1)}, f32[4,1024]{1,0:T(4,128)}, u32[]{:S(2)}) copy-start(f32[4,1024]{1,0:T(4,128)} %get-tuple-element.124) | copy-start | bytes 49156
  274.0 29.5 %copy-start.7 = (f32[1,768]{1,0:T(1,128)S(1)}, f32[1,768]{1,0:T(1,128)}, u32[]{:S(2)}) copy-start(f32[1,768]{1,0:T(1,128)} %get-tuple-element.126) | copy-start | bytes 9220
  380.4 24.4 %copy-start = (f32[2,1024]{1,0:T(2,128)}, f32[2,1024]{1,0:T(2,128)S(1)}, u32[]{:S(2)}) copy-start(f32[2,1024]{1,0:T(2,128)S(1)} %get-tuple-element.258) | copy-start | bytes 24580
